TPU v7x, 32 devices: a whole 2x2x4 slice. The times are simulated.
32 devices in a mesh: groups: 2 (over y), seq: 4 (over z), head: 2 (over x), rep: 2 (over core).
Axes of the slice: x: 2, y: 2, z: 4, core: 2. Of those that a mesh axis runs over, the one named last changes fastest.
Arguments:
- queries: bfloat16 [16384, 2048], P(('groups', 'seq'), ('head', 'rep')), parts along dimension 0, may hold values from -4.5 to 4.5
- key_rows: bfloat16 [16384, 256], P(('groups', 'seq'), 'head'), parts along dimension 0, may hold values from -4.5 to 4.5
- value_rows: bfloat16 [16384, 256], P(('groups', 'seq'), 'head'), parts along dimension 0, may hold values from -8 to 8
- vertical_columns: int32 [4, 1024], P('groups'), parts along dimension 0, may hold values from 0 to 8191, as said below
- slash_offsets: int32 [4, 8], P('groups'), parts along dimension 0, may hold values from 0 to 3968, as said below
Outputs:
- attended: bfloat16 [16384, 2048], P(('groups', 'seq'), ('head', 'rep')), parts along dimension 0
- log_norm: float32 [16, 16384], P(('head', 'rep'), ('groups', 'seq')), parts along dimension 1
There are 2 independent parts, one for each index of `groups`. A program takes and returns all parts, laid end to end along the dimension named above; each array names one. Nothing has to cross between parts.
Inputs may be any that keep to these rules, and one draw needn't show every extreme that they name: `vertical_columns`: each row lists 1024 distinct positions in rising order; each aligned block of 2048 positions holds at most 384 entries of a row, and the first block holds exactly 384. `slash_offsets`: each row lists 8 distinct multiples of 128 in rising order, always including 0 and (31) * 128.
All inputs are finite; a program needn't handle non-finite values.
Results may differ from a plain program's by a relative error of at most 0.0033.
Values may be sent and summed in bfloat16 or wider, within the bound.
No kernel may reach another device: no remote copies, remote signals or barrier semaphores. Data moves between devices by JAX's collectives and lax.ppermute only.
A program may use at most 64 MiB of HBM per device.

v0:
```python
import math

import jax
import jax.numpy as jnp
from jax import lax
from jax.sharding import PartitionSpec as P

BLK = 128
SPAN = 32


def shifted(value, axis, steps):
    count = lax.axis_size(axis)
    leading, last = (max(0, -steps), min(count, count - steps))
    return lax.ppermute(value, axis, [(source, source + steps) for source in range(leading, last)])


def attend_block(query_block, all_keys, all_values, visible):
    scores = jnp.einsum(
        "rgd,kd->grk", query_block, all_keys, preferred_element_type=jnp.float32
    ) * (1.0 / math.sqrt(all_keys.shape[1]))
    masked = jnp.where(visible[None], scores, -1e30)
    row_peak = jnp.max(masked, axis=-1)
    weights = jnp.where(visible[None], jnp.exp(masked - row_peak[..., None]), 0.0)
    row_total = jnp.sum(weights, axis=-1)
    rounded = weights.astype(jnp.bfloat16)
    weighted = (
        jnp.einsum("grk,kd->grd", rounded, all_values, preferred_element_type=jnp.float32)
        / row_total[..., None]
    )
    return (jnp.transpose(weighted.astype(jnp.bfloat16), (1, 0, 2)), row_peak + jnp.log(row_total))


def body(queries, key_rows, value_rows, vertical_columns, slash_offsets):
    seq_count = lax.axis_size("seq")
    seq_index = lax.axis_index("seq")
    head_index = lax.axis_index("head")
    tok_rows = queries.shape[0]
    head_dim = key_rows.shape[1]
    group_heads = queries.shape[1] // head_dim
    nblocks = tok_rows // BLK
    radius = (SPAN + nblocks - 2) // nblocks
    slot_count = 3 * vertical_columns.shape[1] // (2 * seq_count)
    columns = lax.dynamic_index_in_dim(vertical_columns, head_index, 0, keepdims=False)
    shifts = lax.dynamic_index_in_dim(slash_offsets, head_index, 0, keepdims=False) // BLK
    paired = jnp.concatenate([key_rows, value_rows], axis=1)
    shard_starts = jnp.arange(seq_count, dtype=jnp.int32) * tok_rows
    firsts = jnp.sum((columns[None, :] < shard_starts[:, None]).astype(jnp.int32), axis=1)
    sentinel = tok_rows * seq_count
    padded_columns = jnp.concatenate([columns, jnp.full((slot_count,), sentinel, jnp.int32)])
    slot_positions = jnp.take(
        padded_columns, firsts[:, None] + jnp.arange(slot_count, dtype=jnp.int32)[None, :], axis=0
    )
    slot_valid = slot_positions < (shard_starts + tok_rows)[:, None]
    own_positions = lax.dynamic_index_in_dim(slot_positions, seq_index, 0, keepdims=False)
    own_valid = lax.dynamic_index_in_dim(slot_valid, seq_index, 0, keepdims=False)
    local_rows = jnp.where(own_valid, own_positions - seq_index * tok_rows, 0)
    packed = jnp.where(
        own_valid[:, None], jnp.take(paired, local_rows, axis=0), jnp.zeros((), jnp.bfloat16)
    )
    earlier = [shifted(paired, "seq", hop_count) for hop_count in range(radius, 0, -1)]
    gathered = lax.all_gather(packed, "seq", axis=0, tiled=True)
    extended = jnp.concatenate(earlier + [paired], axis=0)
    block_rows = extended.reshape(-1, BLK, 2 * head_dim)
    vert_positions = slot_positions.reshape(-1)
    vert_valid = slot_valid.reshape(-1)
    vert_keys = gathered[:, :head_dim]
    vert_values = gathered[:, head_dim:]
    query_blocks = queries.reshape(nblocks, BLK, group_heads, head_dim)
    offsets_in = jnp.arange(BLK, dtype=jnp.int32)

    def one_block(block_id):
        block_global = seq_index * nblocks + block_id
        tile_valid = block_global - shifts >= 0
        key_tiles = jnp.take(
            block_rows, jnp.maximum(radius * nblocks + block_id - shifts, 0), axis=0
        )
        slash_keys = key_tiles[:, :, :head_dim].reshape(-1, head_dim)
        slash_values = key_tiles[:, :, head_dim:].reshape(-1, head_dim)
        all_keys = jnp.concatenate([slash_keys, vert_keys], axis=0)
        all_values = jnp.concatenate([slash_values, vert_values], axis=0)
        query_pos = block_global * BLK + offsets_in
        slash_mask = (
            tile_valid[None, :, None]
            & (
                (shifts[None, :, None] > 0)
                | (offsets_in[None, None, :] <= offsets_in[:, None, None])
            )
        ).reshape(BLK, -1)
        distance = block_global - vert_positions // BLK
        banned = jnp.any(distance[:, None] == shifts[None, :], axis=1)
        vert_mask = (vert_valid & jnp.logical_not(banned))[None, :] & (
            vert_positions[None, :] <= query_pos[:, None]
        )
        visible = jnp.concatenate([slash_mask, vert_mask], axis=1)
        query_block = lax.dynamic_index_in_dim(query_blocks, block_id, 0, keepdims=False)
        return attend_block(query_block, all_keys, all_values, visible)

    outputs, log_parts = lax.map(one_block, jnp.arange(nblocks, dtype=jnp.int32))
    attended = outputs.reshape(tok_rows, group_heads * head_dim)
    log_norm = jnp.transpose(log_parts, (1, 0, 2)).reshape(group_heads, tok_rows)
    return (attended, log_norm)


def solution(mesh):
    placed = (
        P(("groups", "seq"), ("head", "rep")),
        P(("groups", "seq"), "head"),
        P(("groups", "seq"), "head"),
        P("groups", None),
        P("groups", None),
    )
    return jax.shard_map(
        body,
        mesh=mesh,
        in_specs=placed,
        out_specs=(P(("groups", "seq"), ("head", "rep")), P(("head", "rep"), ("groups", "seq"))),
        check_vma=False,
    )
```

profile of v0, /device:TPU:0, one launch (start us, length us, event | category | flops | bytes accessed | tf_op | source)
XLA Modules:
  0.0 390.4 jit_solution(2418662441399425596)
XLA Ops:
  3.0 7.0 %collective-permute-start = (bf16[2048,256]{1,0:T(8,128)(2,1)S(1)}, bf16[2048,256]{1,0:T(8,128)(2,1)}, u32[]{:S(2)}, u32[]{:S(2)}) collective-permute-start(bf16[2048,256]{1,0:T(8,128)(2,1)S(1)} %constant_dynamic-update-slice_fusion), channel_id=1, source_target_pairs={{0,8},{4,12},{1,9},{5,13},{2,10},{6,14},{3,11},{7,15},{16,24},{20,... | collective-permute-start | bytes 3145736 | tf_op jit(solution)/shard_map/ppermute | solution.py:15
  9.9 4.5 %collective-permute-start.1 = (bf16[2048,256]{1,0:T(8,128)(2,1)S(1)}, bf16[2048,256]{1,0:T(8,128)(2,1)}, u32[]{:S(2)}, u32[]{:S(2)}) collective-permute-start(bf16[2048,256]{1,0:T(8,128)(2,1)S(1)} %constant_dynamic-update-slice_fusion), channel_id=1, source_target_pairs={{0,4},{4,8},{8,12},{1,5},{5,9},{9,13},{2,6},{6,10},{10,14},{3,7},{... | collective-permute-start | bytes 3145736 | tf_op jit(solution)/shard_map/ppermute | solution.py:15
  14.7 8.4 %gather_fusion.1 = s32[1536]{0:T(1024)S(1)} fusion(s32[1408]{0:T(1024)S(1)} %concatenate.30, s32[2048]{0:T(1024)S(1)} %pad_clamp_fusion.1), kind=kCustom, calls=%fused_computation.1 | custom fusion | bytes 18432 | tf_op jit(solution)/shard_map/jit(_take)/gather | solution.py:51
  27.7 2.0 gather_fusion.2
  30.4 2.5 reshape.386
  33.8 60.2 %all_gather.3 = bf16[1536,256]{1,0:T(8,128)(2,1)S(1)} all-gather(bf16[384,256]{1,0:T(8,128)(2,1)S(1)} %select_select_fusion), channel_id=1, replica_groups=mesh['groups'=2,'seq'=4,'head'=2,'rep'=2] {'seq'}, dimensions={0}, use_global_device_ids=true | all-gather | bytes 983040 | tf_op jit(solution)/shard_map/all_gather | solution.py:62
  94.9 3.0 pad_maximum_fusion
  97.9 289.3 %while.17 = (s32[]{:T(128)}, bf16[16,128,4,128]{3,2,1,0:T(4,128)(2,1)}, f32[16,4,128]{2,1,0:T(4,128)}, s32[16]{0:T(128)S(1)}, s32[]{:T(128)}, /*index=5*/s32[8]{...) while((s32[]{:T(128)}, ...), condition=%wide.region_5.6_spmd.clone.clone, body=%wide.region_1.5_spmd.clone.clone.sunk | while | flops 686947520 | bytes 23069680 | solution.py:99
  105.6 2.5 gather_fusion
  110.3 1.9 fusion.55
  123.7 2.5 gather_fusion
  141.7 2.5 gather_fusion
  159.8 2.5 gather_fusion
  177.9 2.5 gather_fusion
  182.6 1.9 fusion.55
  196.0 2.5 gather_fusion
  200.7 1.9 fusion.55
  214.0 2.5 gather_fusion
  232.1 2.5 gather_fusion
  250.2 2.5 gather_fusion
  268.2 2.5 gather_fusion
  273.0 1.9 fusion.55
  286.3 2.5 gather_fusion
  304.4 2.5 gather_fusion
  309.1 1.9 fusion.55
  322.5 2.5 gather_fusion
  340.6 2.5 gather_fusion
  358.7 2.5 gather_fusion
  363.4 1.9 fusion.55
  376.8 2.5 gather_fusion
  381.5 1.9 fusion.55
  387.1 3.3 copy.35
  (407 shorter events, 194.0 us)
Async XLA Ops:
  0.6 13.8 %copy-start = (s32[2,1024]{1,0:T(2,128)S(1)}, s32[2,1024]{1,0:T(2,128)}, u32[]{:S(2)}) copy-start(s32[2,1024]{1,0:T(2,128)} %param.10) | copy-start | bytes 24580
  3.0 91.9 %collective-permute-start = (bf16[2048,256]{1,0:T(8,128)(2,1)S(1)}, bf16[2048,256]{1,0:T(8,128)(2,1)}, u32[]{:S(2)}, u32[]{:S(2)}) collective-permute-start(bf16[2048,256]{1,0:T(8,128)(2,1)S(1)} %constant_dynamic-update-slice_fusion), channel_id=1, source_target_pairs={{0,8},{4,12},{1,9},{5,13},{2,10},{6,14},{3,11},{7,15},{16,24},{20,... | collective-permute-start | bytes 3145736 | tf_op jit(solution)/shard_map/ppermute | solution.py:15
  9.9 84.9 %collective-permute-start.1 = (bf16[2048,256]{1,0:T(8,128)(2,1)S(1)}, bf16[2048,256]{1,0:T(8,128)(2,1)}, u32[]{:S(2)}, u32[]{:S(2)}) collective-permute-start(bf16[2048,256]{1,0:T(8,128)(2,1)S(1)} %constant_dynamic-update-slice_fusion), channel_id=1, source_target_pairs={{0,4},{4,8},{8,12},{1,5},{5,9},{9,13},{2,6},{6,10},{10,14},{3,7},{... | collective-permute-start | bytes 3145736 | tf_op jit(solution)/shard_map/ppermute | solution.py:15
  14.7 12.4 %copy-start.3 = (s32[2,8]{1,0:T(2,128)S(1)}, s32[2,8]{1,0:T(2,128)}, u32[]{:S(2)}) copy-start(s32[2,8]{1,0:T(2,128)} %param.11) | copy-start | bytes 196
  23.2 2.7 copy-start.1
  24.5 5.9 %copy-start.2 = (pred[384]{0:T(512)(128)(4,1)}, pred[384]{0:T(512)(128)(4,1)S(1)}, u32[]{:S(2)}) copy-start(pred[384]{0:T(512)(128)(4,1)S(1)} %compare_reduce_fusion.2) | copy-start | bytes 1156
where the time goes:
time: 395 us; the launch traced here: 390 us
  other arithmetic  115 us (29%)
  local copies, waits for them, and re-layouts  96.8 us (25%)
  blocking collectives  60.2 us (15%)
  matrix products  53.4 us (14%)
  loops' own time  52.3 us (13%)
  starting transfers between devices  11.4 us (3%)
    all_gather x1, blocking collectives, body(): gathered = lax.all_gather(packed, 'seq', axis=0, tiled=True)  60.2 us
    another operation x1, loops' own time, body(): lax.map(one_block, jnp.arange(nblocks, dtype=jnp.int32))  52.3 us
    gather x16, local copies, waits for them, and re-layouts, one_block(): jnp.take(block_rows, jnp.maximum(radius * nblocks + block_id - shifts, 0)...  39.5 us
    dot_general x16, matrix products, attend_block(): jnp.einsum('rgd,kd->grk', query_block, all_keys, preferred_element_type=j...  29.6 us
    dot_general x16, matrix products, attend_block(): jnp.einsum('grk,kd->grd', rounded, all_values, preferred_element_type=jnp...  23.8 us
    and x16, other arithmetic, one_block(): (vert_valid & jnp.logical_not(banned))[None, :]  17 us
    reduce_sum x16, other arithmetic, attend_block(): row_total = jnp.sum(weights, axis=-1)  15.3 us
    reduce_or x16, other arithmetic, one_block(): banned = jnp.any(distance[:, None] == shifts[None, :], axis=1)  12.3 us
  transfers between devices with their start and end apart: 2, of which 0 were waited for; matrix products, arithmetic and copies ran while one was open for 5% of the time, Pallas kernels for 0%

commit v1 on v0

v1 whole, which is shorter than its diff:
```python
import functools
import math

import jax
import jax.numpy as jnp
from jax import lax
from jax.experimental import pallas as pl
from jax.experimental.pallas import tpu as pltpu
from jax.sharding import PartitionSpec as P

BLK = 128
SPAN = 32
LANES = 128
NEG = -1e30
LIMIT = 1e30
LN2 = math.log(2.0)
VMEM_BYTES = 60 * 1024 * 1024
BF16 = jnp.bfloat16
F32 = jnp.float32


def shifted(value, axis, steps):
    count = lax.axis_size(axis)
    leading, last = (max(0, -steps), min(count, count - steps))
    return lax.ppermute(value, axis, [(source, source + steps) for source in range(leading, last)])


def swapped(value):
    return lax.ppermute(value, "rep", [(0, 1), (1, 0)])


def dot(left, right, left_dim, right_dim):
    return lax.dot_general(
        left, right, (((left_dim,), (right_dim,)), ((), ())), preferred_element_type=F32
    )


def sublane_sums(values):
    return jnp.sum(values.reshape(-1, 8, values.shape[1]), axis=0)


def pack_kernel(meta, positions, *refs):
    *parts, out = refs
    slots = positions.shape[0]
    total = jnp.zeros((slots, 2 * LANES), F32)
    where = positions[...]
    row0 = 0
    for mine, other in zip(parts[0::2], parts[1::2]):
        for start in range(0, mine.shape[0], 512):
            hot = jnp.concatenate(
                [
                    jnp.where(
                        where
                        == lax.broadcasted_iota(jnp.int32, where.shape, 1)
                        + (row0 + start + lane0),
                        1.0,
                        0.0,
                    ).astype(BF16)
                    for lane0 in range(0, 512, LANES)
                ],
                axis=1,
            )
            rows = jnp.concatenate(
                [mine[start : start + 512, :], other[start : start + 512, :]], axis=1
            )
            total = total + dot(hot, rows, 1, 0)
        row0 += mine.shape[0]
    packed = total.astype(BF16)
    first, second = packed[:, :LANES], packed[:, LANES:]

    @pl.when(meta[0] == 0)
    def _():
        out[...] = jnp.concatenate([first, second], axis=1)

    @pl.when(meta[0] != 0)
    def _():
        out[...] = jnp.concatenate([second, first], axis=1)


def pack(order, positions, parts):
    slots = positions.shape[0]
    flat = [array for pair in parts for array in pair]
    return pl.pallas_call(
        pack_kernel,
        grid_spec=pltpu.PrefetchScalarGridSpec(
            num_scalar_prefetch=1,
            grid=(1,),
            in_specs=[
                pl.BlockSpec(array.shape, lambda step, meta: (0, 0))
                for array in [positions] + flat
            ],
            out_specs=pl.BlockSpec((slots, 2 * LANES), lambda step, meta: (0, 0)),
        ),
        out_shape=jax.ShapeDtypeStruct((slots, 2 * LANES), BF16),
        compiler_params=pltpu.CompilerParams(vmem_limit_bytes=VMEM_BYTES),
        cost_estimate=pl.CostEstimate(
            flops=2 * slots * 2048 * 256, bytes_accessed=1 << 20, transcendentals=0
        ),
        name="pack_rows",
    )(order, positions, *flat)


def stage_kernel(cfg, meta, q_ref, *refs):
    refs = list(refs)
    nslash = cfg["nslash"]
    heads = q_ref.shape[1] // LANES
    width = heads * BLK
    per_step = cfg["per_step"]
    factor = cfg["factor"]
    first, last = cfg["first"], cfg["last"]
    groups = cfg["groups"]
    sources = cfg["sources"]
    step = pl.program_id(0)
    block0 = meta[nslash]
    core = meta[nslash + 1]

    if not first:
        acc_in, stat_in = refs.pop(0), refs.pop(0)
    vert_refs = [(refs.pop(0), refs.pop(0)) for _ in groups]
    source_refs = [(refs.pop(0), refs.pop(0)) for _ in sources]
    spare_refs = [(refs.pop(0), refs.pop(0)) for _ in cfg["spare"]]
    out_a, out_b = refs.pop(0), refs.pop(0)
    kx, vx, sems = refs.pop(0), refs.pop(0), refs.pop(0)
    if last:
        redo_k, redo_e, redo_acc, redo_stat, redo_sems = refs

    def source_copies(swap):
        copies = []
        for place, ((row0, rows, fixed), (mine, other)) in enumerate(zip(sources, source_refs)):
            targets = (vx, kx) if swap and not fixed else (kx, vx)
            for which, (ref, target) in enumerate(zip((mine, other), targets)):
                copies.append(
                    pltpu.make_async_copy(
                        ref, target.at[pl.ds(row0, rows), :], sems.at[2 * place + which]
                    )
                )
        return copies

    @pl.when(step == 0)
    def _():
        @pl.when(core == 0)
        def _():
            for copy in source_copies(False):
                copy.start()

        @pl.when(core != 0)
        def _():
            for copy in source_copies(True):
                copy.start()

        for copy in source_copies(False):
            copy.wait()

    def tile_rows(index):
        return pl.ds(pl.multiple_of(index * BLK, BLK), BLK)

    def slash_tile(block, place):
        shift = meta[place]
        bias = jnp.where(block0 + block - shift >= 0, 0.0, NEG).astype(F32)
        return jnp.maximum(cfg["own_tile"] + block - shift, 0), bias

    def query_rows(unit):
        rows = slice(unit * BLK, (unit + 1) * BLK)
        return jnp.concatenate(
            [q_ref[rows, h * LANES : (h + 1) * LANES] for h in range(heads)], axis=0
        )

    def marked(query, block):
        lane = lax.broadcasted_iota(jnp.int32, (query.shape[0], LANES), 1)
        return jnp.concatenate([query, jnp.where(lane == block, 1.0, 0.0).astype(BF16)], axis=1)

    def causal(scores):
        key_at = lax.broadcasted_iota(jnp.int32, scores.shape, 0)
        query_at = lax.broadcasted_iota(jnp.int32, scores.shape, 1) % BLK
        return jnp.where(key_at <= query_at, scores, NEG)

    def finish(unit, acc, sums, peak):
        total = jnp.sum(sums, axis=0, keepdims=True)
        result = (acc / total).astype(BF16)
        norm = peak[:1] * LN2 + jnp.log(total)
        for h in range(heads):
            part = slice(h * LANES, (h + 1) * LANES)
            out_a[unit * BLK : (unit + 1) * BLK, part] = result[:, part].T
            out_b[h : h + 1, unit * BLK : (unit + 1) * BLK] = norm[:, part]
        return total

    def one_unit(unit, tiles, with_slash):
        block = step * per_step + unit
        query = query_rows(unit)
        rows = slice(unit * BLK, (unit + 1) * BLK)
        stat = 2 * 8 * unit
        acc = sums = None
        if first:
            own = tile_rows(cfg["own_tile"] + block)
            scores = causal(dot(kx[own, :], query, 1, 1)) * factor
            peak = jnp.broadcast_to(jnp.max(scores, axis=0, keepdims=True), (8, width))
            weights = jnp.exp2(scores - peak[:1])
            sums = sublane_sums(weights)
            acc = dot(vx[own, :], weights.astype(BF16), 0, 0)
        else:
            sums = stat_in[stat : stat + 8, :]
            peak = stat_in[stat + 8 : stat + 16, :]
        base = peak[:1]
        if sum(tiles):
            keys = jnp.concatenate(
                [
                    jnp.concatenate([kv[: n * BLK, :LANES], mark[: n * BLK, :]], axis=1)
                    for n, (kv, mark) in zip(tiles, vert_refs)
                    if n
                ],
                axis=0,
            )
            values = jnp.concatenate(
                [kv[: n * BLK, LANES:] for n, (kv, _) in zip(tiles, vert_refs) if n], axis=0
            )
            weights = jnp.exp2(dot(keys, marked(query, block), 1, 1) * factor - base)
            sums = sums + sublane_sums(weights)
            more = dot(values, weights.astype(BF16), 0, 0)
            acc = more if acc is None else acc + more
        if with_slash:
            chosen = [slash_tile(block, place) for place in range(1, nslash)]
            keys = jnp.concatenate([kx[tile_rows(index), :] for index, _ in chosen], axis=0)
            values = jnp.concatenate([vx[tile_rows(index), :] for index, _ in chosen], axis=0)
            scores = dot(keys, query, 1, 1)
            parts = []
            for place, (_, bias) in enumerate(chosen):
                weights = jnp.exp2(
                    scores[place * BLK : (place + 1) * BLK, :] * factor + (bias - base)
                )
                sums = sums + sublane_sums(weights)
                parts.append(weights.astype(BF16))
            more = dot(values, jnp.concatenate(parts, axis=0), 0, 0)
            acc = more if acc is None else acc + more
        if not first:
            acc = acc_in[rows, :] if acc is None else acc_in[rows, :] + acc
        if last:
            return finish(unit, acc, sums, peak)
        out_a[rows, :] = acc
        out_b[stat : stat + 8, :] = sums
        out_b[stat + 8 : stat + 16, :] = peak
        return None

    def redo(unit):
        block = step * per_step + unit
        query = query_rows(unit)
        copies = []
        row0 = 0
        for place, (kv, mark) in enumerate(spare_refs):
            part = pl.ds(row0, kv.shape[0])
            copies.append(pltpu.make_async_copy(kv, redo_k.at[part, :], redo_sems.at[2 * place]))
            copies.append(
                pltpu.make_async_copy(mark, redo_e.at[part, :], redo_sems.at[2 * place + 1])
            )
            row0 += kv.shape[0]
        for copy in copies:
            copy.start()
        for copy in copies:
            copy.wait()
        redo_acc[...] = jnp.zeros_like(redo_acc)
        redo_stat[0:8, :] = jnp.zeros((8, width), F32)
        redo_stat[8:16, :] = jnp.full((8, width), NEG, F32)

        def merge(scores, values):
            peak = redo_stat[8:16, :]
            high = jnp.maximum(peak, jnp.max(scores, axis=0, keepdims=True))
            weights = jnp.where(scores > 1e-3 * NEG, jnp.exp2(scores - high[:1]), 0.0)
            shrink = jnp.exp2(peak - high)
            redo_stat[0:8, :] = redo_stat[0:8, :] * shrink + sublane_sums(weights)
            redo_stat[8:16, :] = high
            redo_acc[...] = redo_acc[...] * shrink[:1] + dot(values, weights.astype(BF16), 0, 0)

        def slash_step(place, carry):
            index, bias = slash_tile(block, place)
            scores = dot(kx[tile_rows(index), :], query, 1, 1) * factor + bias
            key_at = lax.broadcasted_iota(jnp.int32, scores.shape, 0)
            query_at = lax.broadcasted_iota(jnp.int32, scores.shape, 1) % BLK
            reach = jnp.where(meta[place] > 0, BLK, 0)
            merge(jnp.where(key_at <= query_at + reach, scores, NEG), vx[tile_rows(index), :])
            return carry

        def vert_step(tile, carry):
            here = tile_rows(tile)
            keys = jnp.concatenate([redo_k[here, :LANES], redo_e[here, :]], axis=1)
            merge(dot(keys, marked(query, block), 1, 1) * factor, redo_k[here, LANES:])
            return carry

        lax.fori_loop(0, nslash, slash_step, 0)
        lax.fori_loop(0, redo_k.shape[0] // BLK, vert_step, 0)
        finish(unit, redo_acc[...], redo_stat[0:8, :], redo_stat[8:16, :])

    def whole_step(tiles):
        totals = [one_unit(unit, tiles, cfg["slash"]) for unit in range(per_step)]
        if last:
            for unit, total in enumerate(totals):
                worst = jnp.max(jnp.where(total < LIMIT, 0.0, 1.0))

                @pl.when(worst > 0.0)
                def _():
                    redo(unit)

    small = [min(n, 2) for n in groups]
    limited = [g for g, n in enumerate(groups) if n > 2 and cfg["counted"][g]]
    if limited:
        fits = functools.reduce(
            jnp.logical_and, [meta[nslash + 2 + g] <= 2 * BLK for g in limited]
        )
        few = [small[g] if g in limited else n for g, n in enumerate(groups)]

        @pl.when(fits)
        def _():
            whole_step(few)

        @pl.when(jnp.logical_not(fits))
        def _():
            whole_step(groups)
    else:
        whole_step(groups)


def stage(meta, queries, state, verts, counted, sources, spare, *, nslash, first, last, slash, own_tile, tiles, per_step=2):
    rows, columns = queries.shape
    heads = columns // LANES
    width = heads * BLK
    nblocks = rows // BLK
    cfg = dict(
        nslash=nslash,
        per_step=per_step,
        factor=1.0 / (math.sqrt(LANES) * LN2),
        first=first,
        last=last,
        slash=slash,
        own_tile=own_tile,
        groups=[kv.shape[0] // BLK for kv, _ in verts],
        counted=counted,
        sources=[(row0, mine.shape[0], fixed) for row0, fixed, mine, _ in sources],
        spare=[kv.shape for kv, _ in spare],
    )

    def moving(block_rows):
        return pl.BlockSpec((block_rows * per_step, width), lambda step, meta: (step, 0))

    def whole(array):
        return pl.BlockSpec(array.shape, lambda step, meta: (0, 0))

    anywhere = pl.BlockSpec(memory_space=pl.ANY)
    operands, specs = [queries], [pl.BlockSpec((BLK * per_step, columns), lambda s, m: (s, 0))]
    if not first:
        operands += list(state)
        specs += [moving(BLK), moving(16)]
    for pair in verts:
        operands += list(pair)
        specs += [whole(array) for array in pair]
    for _, _, mine, other in sources:
        operands += [mine, other]
        specs += [anywhere, anywhere]
    for pair in spare:
        operands += list(pair)
        specs += [anywhere, anywhere]
    scratch = [
        pltpu.VMEM((tiles * BLK, LANES), BF16),
        pltpu.VMEM((tiles * BLK, LANES), BF16),
        pltpu.SemaphoreType.DMA((2 * len(sources),)),
    ]
    if last:
        out_shape = [
            jax.ShapeDtypeStruct((rows, columns), BF16),
            jax.ShapeDtypeStruct((heads, rows), F32),
        ]
        out_specs = [
            pl.BlockSpec((BLK * per_step, columns), lambda s, m: (s, 0)),
            pl.BlockSpec((heads, BLK * per_step), lambda s, m: (0, s)),
        ]
        spare_rows = sum(kv.shape[0] for kv, _ in spare)
        scratch += [
            pltpu.VMEM((spare_rows, 2 * LANES), BF16),
            pltpu.VMEM((spare_rows, LANES), BF16),
            pltpu.VMEM((BLK, width), F32),
            pltpu.VMEM((16, width), F32),
            pltpu.SemaphoreType.DMA((2 * len(spare),)),
        ]
    else:
        out_shape = [
            jax.ShapeDtypeStruct((nblocks * BLK, width), F32),
            jax.ShapeDtypeStruct((nblocks * 16, width), F32),
        ]
        out_specs = [moving(BLK), moving(16)]
    keys = sum(kv.shape[0] for kv, _ in verts) + (nslash - 1) * BLK * slash + BLK * first
    return pl.pallas_call(
        functools.partial(stage_kernel, cfg),
        grid_spec=pltpu.PrefetchScalarGridSpec(
            num_scalar_prefetch=1,
            grid=(nblocks // per_step,),
            in_specs=specs,
            out_specs=out_specs,
            scratch_shapes=scratch,
        ),
        out_shape=out_shape,
        compiler_params=pltpu.CompilerParams(vmem_limit_bytes=VMEM_BYTES),
        cost_estimate=pl.CostEstimate(
            flops=8 * rows * heads * keys * LANES,
            bytes_accessed=8 << 20,
            transcendentals=rows * heads * keys,
        ),
        name="attend_stage",
    )(meta, *operands)


def body(queries, key_rows, value_rows, vertical_columns, slash_offsets):
    seq_count = lax.axis_size("seq")
    seq_index = lax.axis_index("seq")
    head_index = lax.axis_index("head")
    core = lax.axis_index("rep")
    tok_rows = queries.shape[0]
    nblocks = tok_rows // BLK
    radius = (SPAN + nblocks - 2) // nblocks
    nvert = vertical_columns.shape[1]
    nslash = slash_offsets.shape[1]
    slot_count = 3 * nvert // (2 * seq_count)
    slot_pad = -(-slot_count // BLK) * BLK

    payload = jnp.where(core == 0, key_rows, value_rows)
    half = tok_rows // 2
    order = [1, 0]
    hops = [[None, None] for _ in range(radius)]
    for piece in order:
        moved = payload[piece * half : (piece + 1) * half]
        for hop in range(radius):
            moved = shifted(moved, "seq", 1)
            hops[hop][piece] = (moved, swapped(moved))

    columns = lax.dynamic_index_in_dim(vertical_columns, head_index, 0, keepdims=False)
    shifts = lax.dynamic_index_in_dim(slash_offsets, head_index, 0, keepdims=False) // BLK
    padded = jnp.concatenate([columns, jnp.full((slot_pad,), tok_rows * seq_count, jnp.int32)])
    own_blocks = seq_index * nblocks + jnp.arange(LANES, dtype=jnp.int32)

    def slots_of(distance, count):
        start = (seq_index - distance) * tok_rows
        ahead = jnp.sum((columns < start).astype(jnp.int32))
        listed = lax.dynamic_slice_in_dim(padded, ahead, count, 0)
        valid = (listed < start + tok_rows) & (start >= 0)
        return (listed, valid, jnp.where(valid, listed - start, -1))

    def marks_of(listed, valid):
        distance = own_blocks[None, :] - (listed // BLK)[:, None]
        seen = valid[:, None] & (distance > 0)
        for place in range(nslash):
            seen = seen & (distance != shifts[place])
        return jnp.where(seen, 0.0, NEG).astype(BF16)

    near = [slots_of(distance, slot_pad) for distance in range(radius + 1)]
    near_marks = [marks_of(listed, valid) for listed, valid, _ in near]
    near_places = [
        jnp.broadcast_to(place[:, None], (slot_pad, LANES)) for _, _, place in near
    ]
    counts = [jnp.sum(valid.astype(jnp.int32)) for _, valid, _ in near]

    none = jnp.zeros((1,), jnp.int32)
    core_meta = jnp.reshape(core, (1,)).astype(jnp.int32)
    own_pack = pack(none, near_places[0], [(key_rows, value_rows)])
    own_verts = (own_pack, near_marks[0])

    far_verts = []
    distances = list(range(radius + 1, seq_count))
    if distances:
        far_payload = jnp.where(
            core == 0, own_pack[:slot_count, :LANES], own_pack[:slot_count, LANES:]
        )
        rows, listed, valid = [], [], []
        for distance in distances:
            mine = shifted(far_payload, "seq", distance)
            other = swapped(mine)
            rows.append(
                jnp.where(
                    core == 0,
                    jnp.concatenate([mine, other], axis=1),
                    jnp.concatenate([other, mine], axis=1),
                )
            )
            at, ok, _ = slots_of(distance, slot_count)
            listed.append(at)
            valid.append(ok)
        extra = -len(distances) * slot_count % BLK
        far_rows = jnp.pad(jnp.concatenate(rows, axis=0), ((0, extra), (0, 0)))
        far_marks = marks_of(
            jnp.pad(jnp.concatenate(listed), (0, extra)),
            jnp.pad(jnp.concatenate(valid), (0, extra)),
        )
        far_verts = [(far_rows, far_marks)]

    base_meta = jnp.concatenate(
        [
            shifts.astype(jnp.int32),
            jnp.reshape(seq_index * nblocks, (1,)).astype(jnp.int32),
            core_meta,
        ]
    )
    meta = jnp.concatenate([base_meta] + [jnp.reshape(count, (1,)) for count in counts])

    own_source = [(0, True, key_rows, value_rows)]
    state = stage(
        meta[: nslash + 3], queries, None, [own_verts], [True], own_source, [],
        nslash=nslash, first=True, last=False, slash=False, own_tile=0, tiles=nblocks,
    )
    hop_verts = [
        (pack(core_meta, near_places[hop + 1], hops[hop]), near_marks[hop + 1])
        for hop in range(radius)
    ]
    sources = []
    for hop in range(radius):
        for piece in range(2):
            row0 = (radius - 1 - hop) * tok_rows + piece * half
            sources.append((row0, False) + hops[hop][piece])
    sources.append((radius * tok_rows, True, key_rows, value_rows))
    rest = hop_verts + far_verts
    return tuple(
        stage(
            jnp.concatenate([base_meta, meta[nslash + 3 :], jnp.zeros((1,), jnp.int32)]),
            queries, state, rest, [True] * radius + [False] * len(far_verts), sources,
            [own_verts] + rest,
            nslash=nslash, first=False, last=True, slash=True, own_tile=radius * nblocks,
            tiles=(radius + 1) * nblocks,
        )
    )


def solution(mesh):
    placed = (
        P(("groups", "seq"), ("head", "rep")),
        P(("groups", "seq"), "head"),
        P(("groups", "seq"), "head"),
        P("groups", None),
        P("groups", None),
    )
    return jax.shard_map(
        body,
        mesh=mesh,
        in_specs=placed,
        out_specs=(P(("groups", "seq"), ("head", "rep")), P(("head", "rep"), ("groups", "seq"))),
        check_vma=False,
    )
```

time: 395 us -> 87.5 us (0.22)
  other arithmetic: 115 us -> 12.2 us
  local copies, waits for them, and re-layouts: 96.8 us -> 5.71 us
  blocking collectives: 60.2 us -> 0 us
  matrix products: 53.4 us -> 0 us
  loops' own time: 52.3 us -> 0 us
  Pallas kernels: 0 us -> 43.8 us
  between operations: 0.75 us -> 8.56 us
  starting transfers between devices: 11.4 us -> 16.3 us
    all_gather x1 -> x0, blocking collectives: 60.2 us -> none  [body(): gathered = lax.all_gather(packed, 'seq', axis=0, tiled=True)]
    dot_general x32 -> x0, matrix products: 53.4 us -> none  [the longest x16 29.6 us: attend_block(): jnp.einsum('rgd,kd->grk', query_block, all_keys, preferred_element_type=j...]
    another operation x1 -> x0, loops' own time: 52.3 us -> none  [body(): lax.map(one_block, jnp.arange(nblocks, dtype=jnp.int32))]
    gather x19 -> x0, local copies, waits for them, and re-layouts: 50 us -> none  [the longest x16 39.5 us: one_block(): jnp.take(block_rows, jnp.maximum(radius * nblocks + block_id - shifts, 0)...]
    pallas_call x0 -> x5, Pallas kernels: none -> 43.8 us  [the longest x2 36.3 us: stage(): pl.pallas_call(functools.partial(stage_kernel, cfg), grid_spec=pltpu.Pref...]
    and x49 -> x1, other arithmetic: 33.7 us -> 0.08 us  [slots_of(): valid = (listed < start + tok_rows) & (start >= 0)]
    reduce_sum x17 -> x3, other arithmetic: 15.5 us -> 2.02 us  [the longest x2 1.3 us: body(): counts = [jnp.sum(valid.astype(jnp.int32)) for _, valid, _ in near]]
    reduce_or x16 -> x0, other arithmetic: 12.3 us -> none  [one_block(): banned = jnp.any(distance[:, None] == shifts[None, :], axis=1)]
  transfers between devices with their start and end apart: 2 -> 10, of which waited for: 0 -> 0; matrix products, arithmetic and copies ran while one was open for 5% -> 16% of each run, Pallas kernels for 0% -> 17%
where the time goes in v1:
time: 87.5 us; the launch traced here: 86.7 us
  Pallas kernels  43.8 us (50%)
  starting transfers between devices  16.3 us (19%)
  other arithmetic  12.2 us (14%)
  between operations  8.56 us (10%)
  local copies, waits for them, and re-layouts  5.71 us (7%)
    pallas_call x2, Pallas kernels, stage(): pl.pallas_call(functools.partial(stage_kernel, cfg), grid_spec=pltpu.Pref...  36.3 us
    ppermute x5, starting transfers between devices, shifted(): lax.ppermute(value, axis, [(source, source + steps) for source in range(l...  15.1 us
    pallas_call x3, Pallas kernels, pack(): pl.pallas_call(pack_kernel, grid_spec=pltpu.PrefetchScalarGridSpec(num_sc...  7.56 us
    convert_element_type x1, other arithmetic, marks_of(): return jnp.where(seen, 0.0, NEG).astype(BF16)  6.89 us
    broadcast_in_dim x3, local copies, waits for them, and re-layouts, body(): jnp.broadcast_to(place[:, None], (slot_pad, LANES))  2.46 us
    concatenate x1, local copies, waits for them, and re-layouts, body(): jnp.concatenate([base_meta, meta[nslash + 3:], jnp.zeros((1,), jnp.int32)])  1.84 us
  transfers between devices with their start and end apart: 10, of which 0 were waited for; matrix products, arithmetic and copies ran while one was open for 16% of the time, Pallas kernels for 17%

profile of v1, /device:TPU:0, one launch (start us, length us, event | category | flops | bytes accessed | tf_op | source)
XLA Modules:
  0.0 86.7 jit_solution(9390747983041087772)
XLA Ops:
  0.7 0.6 copy-done
  1.3 0.7 convert_reduce_fusion
  9.7 0.1 add_select_fusion
  9.8 0.8 broadcast_in_dim.27.positions
  10.6 2.5 %pack_rows.3.refs_0_.refs_18_ = bf16[384,256]{1,0:T(8,128)(2,1)} custom-call(s32[1]{0:T(128)} %constant.87.clone.1.meta, s32[384,128]{1,0:T(8,128)} %broadcast_in_dim.27.positions, bf16[2048,128]{1,0:T(8,128)(2,1)} %refs_16_.1, bf16[2048,128]{1,0:T(8,128)(2,1)} %refs_17_.1), custom_call_target="tpu_custom_call" | custom-call | flops 402653184 | bytes 1048576 | tf_op jit(solution)/shard_map/pack_rows/pallas_call | solution.py:83
  13.2 1.0 %slice_select_fusion = bf16[384,128]{1,0:T(8,128)(2,1)S(1)} fusion(bf16[384,256]{1,0:T(8,128)(2,1)} %pack_rows.3.refs_0_.refs_18_, pred[]{:T(512)S(6)} %eq.2), kind=kLoop, calls=%fused_computation.78 | loop fusion | flops 49152 | bytes 294913 | tf_op jit(solution)/shard_map/jit(_where)/select_n | solution.py:465
  14.1 7.0 %collective-permute-start.8 = (bf16[384,128]{1,0:T(8,128)(2,1)S(1)}, bf16[384,128]{1,0:T(8,128)(2,1)S(1)}, u32[]{:S(2)}, u32[]{:S(2)}) collective-permute-start(bf16[384,128]{1,0:T(8,128)(2,1)S(1)} %slice_select_fusion), channel_id=1, source_target_pairs={{0,12},{1,13},{2,14},{3,15},{16,28},{17,29},{18,30},{19,31}} | collective-permute-start | bytes 294920 | tf_op jit(solution)/shard_map/ppermute | solution.py:25
  21.1 0.1 broadcast_select_fusion
  21.2 1.3 %collective-permute-start.2 = (bf16[1024,128]{1,0:T(8,128)(2,1)S(1)}, bf16[1024,128]{1,0:T(8,128)(2,1)S(1)}, u32[]{:S(2)}, u32[]{:S(2)}) collective-permute-start(bf16[1024,128]{1,0:T(8,128)(2,1)S(1)} %get-tuple-element.16), channel_id=1, source_target_pairs={{0,4},{4,8},{8,12},{1,5},{5,9},{9,13},{2,6},{6,10},{10,14},{3,7},{... | collective-permute-start | bytes 786440 | tf_op jit(solution)/shard_map/ppermute | solution.py:25
  22.5 1.3 %collective-permute-start = (bf16[1024,128]{1,0:T(8,128)(2,1)S(1)}, bf16[1024,128]{1,0:T(8,128)(2,1)S(1)}, u32[]{:S(2)}, u32[]{:S(2)}) collective-permute-start(bf16[1024,128]{1,0:T(8,128)(2,1)S(1)} %get-tuple-element.17), channel_id=1, source_target_pairs={{0,4},{4,8},{8,12},{1,5},{5,9},{9,13},{2,6},{6,10},{10,14},{3,7},{... | collective-permute-start | bytes 786440 | tf_op jit(solution)/shard_map/ppermute | solution.py:25
  23.9 0.7 fusion.45
  24.6 0.1 compare_and_fusion
  24.6 0.1 subtract_select_fusion.1
  24.7 0.7 convert_reduce_fusion.4
  25.4 1.3 %pad_add_fusion.meta = s32[11]{0:T(128)} fusion(s32[1]{0:T(128)} %bitcast.6, s32[1]{0:T(128)} %bitcast.2.meta, s32[1]{0:T(128)} %bitcast.1, s32[8]{0:T(128)S(1)} %and_select_fusion), kind=kLoop, calls=%fused_computation.129 | loop fusion | flops 33 | bytes 88 | tf_op jit(solution)/shard_map/concatenate | solution.py:497
  26.7 6.9 %select_convert_fusion = (bf16[384,128]{1,0:T(8,128)(2,1)}, bf16[384,128]{1,0:T(8,128)(2,1)}, bf16[384,128]{1,0:T(8,128)(2,1)}, bf16[384,128]{1,0:T(8,128)(2,1)}) fusion(s32[384]{0:T(512)S(1)} %get-tuple-element.18, s32[]{:T(128)} %bitcast.14, s32[]{:T(128)} %bitcast.13, s32[]{:T(128)} %bitcast.12, s32[]{:T(128)} %bitcast.11, s32[]{:T(128)} %bitcast.10, ...), kind=kLoop, calls=%fused_computation.38 | loop fusion | flops 4128768 | bytes 401440 | tf_op jit(solution)/shard_map/convert_element_type | solution.py:448
  33.6 3.6 %collective-permute-start.6 = (bf16[1024,128]{1,0:T(8,128)(2,1)S(1)}, bf16[1024,128]{1,0:T(8,128)(2,1)S(1)}, u32[]{:S(2)}, u32[]{:S(2)}) collective-permute-start(bf16[1024,128]{1,0:T(8,128)(2,1)S(1)} %collective-permute-done.2.refs_2_.refs_10_), channel_id=1, source_target_pairs={{0,4},{4,8},{8,12},{1,5},{5,9},{9,13},{2,6},{6,10},{10,14},{3,7},{... | collective-permute-start | bytes 786440 | tf_op jit(solution)/shard_map/ppermute | solution.py:25
  37.2 0.1 collective-permute-start.3
  37.3 1.9 %collective-permute-start.4 = (bf16[1024,128]{1,0:T(8,128)(2,1)S(1)}, bf16[1024,128]{1,0:T(8,128)(2,1)S(1)}, u32[]{:S(2)}, u32[]{:S(2)}) collective-permute-start(bf16[1024,128]{1,0:T(8,128)(2,1)S(1)} %collective-permute-done.refs_0_.refs_8_), channel_id=1, source_target_pairs={{0,4},{4,8},{8,12},{1,5},{5,9},{9,13},{2,6},{6,10},{10,14},{3,7},{... | collective-permute-start | bytes 786440 | tf_op jit(solution)/shard_map/ppermute | solution.py:25
  39.3 0.3 collective-permute-start.1
  39.5 12.6 %attend_stage.2 = (f32[2048,512]{1,0:T(8,128)}, f32[256,512]{1,0:T(8,128)}) custom-call(s32[11]{0:T(128)} %pad_add_fusion.meta, bf16[2048,512]{1,0:T(8,128)(2,1)} %q_ref.3, bf16[384,256]{1,0:T(8,128)(2,1)} %pack_rows.3.refs_0_.refs_18_, bf16[384,128]{1,0:T(8,128)(2,1)} %get-tuple-element.29.refs_1_.refs_19_, bf16[2048,128]{1,0:T(8,128)(2,1)} %refs_16_.1, ...), custom_call_target="tpu_custom_call" | custom-call | flops 4294967296 | bytes 8388608 | tf_op jit(solution)/shard_map/attend_stage/pallas_call | solution.py:388
  52.1 0.3 collective-permute-start.9
  52.5 0.2 collective-permute-start.7
  52.7 0.3 collective-permute-start.5
  53.0 0.6 convert_reduce_fusion.6
  53.6 1.8 %concatenate.22.meta = s32[13]{0:T(128)} concatenate(s32[8]{0:T(128)S(1)} %and_select_fusion, s32[1]{0:T(128)} %bitcast.1, s32[1]{0:T(128)} %bitcast.2.meta, s32[1]{0:T(128)} %bitcast.4, s32[1]{0:T(128)} %bitcast.5, s32[1]{0:T(128)} %constant.87.clone.1.meta), dimensions={0} | concatenate | bytes 104 | tf_op jit(solution)/shard_map/concatenate | solution.py:517
  55.5 0.7 maximum_select_fusion.refs_6_.refs_24_
  56.2 0.8 broadcast_in_dim.30.positions
  57.1 2.5 %pack_rows.4.refs_2_.refs_20_ = bf16[384,256]{1,0:T(8,128)(2,1)} custom-call(s32[1]{0:T(128)} %bitcast.2.meta, s32[384,128]{1,0:T(8,128)} %broadcast_in_dim.30.positions, bf16[1024,128]{1,0:T(8,128)(2,1)} %copy-done.4, bf16[1024,128]{1,0:T(8,128)(2,1)} %copy-done.8, bf16[1024,128]{1,0:T(8,128)(2,1)} %copy-done.3, bf16[1024,128]{1,0:T(8,128)(2,1)} %copy-done.6), custom_call_target="tpu_custom_call" | custom-call | flops 402653184 | bytes 1048576 | tf_op jit(solution)/shard_map/pack_rows/pallas_call | solution.py:83
  59.6 0.8 broadcast_in_dim.56.positions
  60.5 2.5 %pack_rows.5.refs_4_.refs_22_ = bf16[384,256]{1,0:T(8,128)(2,1)} custom-call(s32[1]{0:T(128)} %bitcast.2.meta, s32[384,128]{1,0:T(8,128)} %broadcast_in_dim.56.positions, bf16[1024,128]{1,0:T(8,128)(2,1)} %copy-done.7, bf16[1024,128]{1,0:T(8,128)(2,1)} %copy-done.10, bf16[1024,128]{1,0:T(8,128)(2,1)} %copy-done.5, bf16[1024,128]{1,0:T(8,128)(2,1)} %copy-done.9), custom_call_target="tpu_custom_call" | custom-call | flops 402653184 | bytes 1048576 | tf_op jit(solution)/shard_map/pack_rows/pallas_call | solution.py:83
  63.0 23.7 %attend_stage.3 = (bf16[2048,512]{1,0:T(8,128)(2,1)}, f32[4,2048]{1,0:T(4,128)}) custom-call(s32[13]{0:T(128)} %concatenate.22.meta, bf16[2048,512]{1,0:T(8,128)(2,1)} %q_ref.3, f32[2048,512]{1,0:T(8,128)} %get-tuple-element.4.refs_0_, f32[256,512]{1,0:T(8,128)} %get-tuple-element.5.refs_1_, bf16[384,256]{1,0:T(8,128)(2,1)} %pack_rows.4.refs_2_.refs_20_, ...), custom_call_target="tpu_custom_call" | custom-call | flops 17179869184 | bytes 8388608 | tf_op jit(solution)/shard_map/attend_stage/pallas_call | solution.py:388
  (37 shorter events, 0.1 us)
Async XLA Ops:
  0.6 0.7 copy-start
  0.6 20.4 %copy-start.2 = (bf16[2048,128]{1,0:T(8,128)(2,1)S(1)}, bf16[2048,128]{1,0:T(8,128)(2,1)}, u32[]{:S(2)}) copy-start(bf16[2048,128]{1,0:T(8,128)(2,1)} %refs_17_.1) | copy-start | bytes 1572868
  0.7 20.4 %copy-start.1 = (bf16[2048,128]{1,0:T(8,128)(2,1)S(1)}, bf16[2048,128]{1,0:T(8,128)(2,1)}, u32[]{:S(2)}) copy-start(bf16[2048,128]{1,0:T(8,128)(2,1)} %refs_16_.1) | copy-start | bytes 1572868
  10.6 13.2 %copy-start.11 = (s32[2,8]{1,0:T(2,128)S(1)}, s32[2,8]{1,0:T(2,128)}, u32[]{:S(2)}) copy-start(s32[2,8]{1,0:T(2,128)} %param.9) | copy-start | bytes 196
  14.1 38.0 %collective-permute-start.8 = (bf16[384,128]{1,0:T(8,128)(2,1)S(1)}, bf16[384,128]{1,0:T(8,128)(2,1)S(1)}, u32[]{:S(2)}, u32[]{:S(2)}) collective-permute-start(bf16[384,128]{1,0:T(8,128)(2,1)S(1)} %slice_select_fusion), channel_id=1, source_target_pairs={{0,12},{1,13},{2,14},{3,15},{16,28},{17,29},{18,30},{19,31}} | collective-permute-start | bytes 294920 | tf_op jit(solution)/shard_map/ppermute | solution.py:25
  21.2 12.4 %collective-permute-start.2 = (bf16[1024,128]{1,0:T(8,128)(2,1)S(1)}, bf16[1024,128]{1,0:T(8,128)(2,1)S(1)}, u32[]{:S(2)}, u32[]{:S(2)}) collective-permute-start(bf16[1024,128]{1,0:T(8,128)(2,1)S(1)} %get-tuple-element.16), channel_id=1, source_target_pairs={{0,4},{4,8},{8,12},{1,5},{5,9},{9,13},{2,6},{6,10},{10,14},{3,7},{... | collective-permute-start | bytes 786440 | tf_op jit(solution)/shard_map/ppermute | solution.py:25
  22.5 14.8 %collective-permute-start = (bf16[1024,128]{1,0:T(8,128)(2,1)S(1)}, bf16[1024,128]{1,0:T(8,128)(2,1)S(1)}, u32[]{:S(2)}, u32[]{:S(2)}) collective-permute-start(bf16[1024,128]{1,0:T(8,128)(2,1)S(1)} %get-tuple-element.17), channel_id=1, source_target_pairs={{0,4},{4,8},{8,12},{1,5},{5,9},{9,13},{2,6},{6,10},{10,14},{3,7},{... | collective-permute-start | bytes 786440 | tf_op jit(solution)/shard_map/ppermute | solution.py:25
  33.6 18.5 %copy-start.3 = (bf16[1024,128]{1,0:T(8,128)(2,1)}, bf16[1024,128]{1,0:T(8,128)(2,1)S(1)}, u32[]{:S(2)}) copy-start(bf16[1024,128]{1,0:T(8,128)(2,1)S(1)} %collective-permute-done.2.refs_2_.refs_10_) | copy-start | bytes 786436
  33.6 18.9 %collective-permute-start.6 = (bf16[1024,128]{1,0:T(8,128)(2,1)S(1)}, bf16[1024,128]{1,0:T(8,128)(2,1)S(1)}, u32[]{:S(2)}, u32[]{:S(2)}) collective-permute-start(bf16[1024,128]{1,0:T(8,128)(2,1)S(1)} %collective-permute-done.2.refs_2_.refs_10_), channel_id=1, source_target_pairs={{0,4},{4,8},{8,12},{1,5},{5,9},{9,13},{2,6},{6,10},{10,14},{3,7},{... | collective-permute-start | bytes 786440 | tf_op jit(solution)/shard_map/ppermute | solution.py:25
  37.2 19.0 %collective-permute-start.3 = (bf16[1024,128]{1,0:T(8,128)(2,1)S(1)}, bf16[1024,128]{1,0:T(8,128)(2,1)S(1)}, u32[]{:S(2)}, u32[]{:S(2)}) collective-permute-start(bf16[1024,128]{1,0:T(8,128)(2,1)S(1)} %collective-permute-done.2.refs_2_.refs_10_), channel_id=1, source_target_pairs={{0,1},{1,0},{2,3},{3,2},{4,5},{5,4},{6,7},{7,6},{8,9},{9,8},{10,11... | collective-permute-start | bytes 786440 | tf_op jit(solution)/shard_map/ppermute | solution.py:29
  37.3 14.8 %copy-start.4 = (bf16[1024,128]{1,0:T(8,128)(2,1)}, bf16[1024,128]{1,0:T(8,128)(2,1)S(1)}, u32[]{:S(2)}) copy-start(bf16[1024,128]{1,0:T(8,128)(2,1)S(1)} %collective-permute-done.refs_0_.refs_8_) | copy-start | bytes 786436
  37.3 15.4 %collective-permute-start.4 = (bf16[1024,128]{1,0:T(8,128)(2,1)S(1)}, bf16[1024,128]{1,0:T(8,128)(2,1)S(1)}, u32[]{:S(2)}, u32[]{:S(2)}) collective-permute-start(bf16[1024,128]{1,0:T(8,128)(2,1)S(1)} %collective-permute-done.refs_0_.refs_8_), channel_id=1, source_target_pairs={{0,4},{4,8},{8,12},{1,5},{5,9},{9,13},{2,6},{6,10},{10,14},{3,7},{... | collective-permute-start | bytes 786440 | tf_op jit(solution)/shard_map/ppermute | solution.py:25
  39.3 17.0 %collective-permute-start.1 = (bf16[1024,128]{1,0:T(8,128)(2,1)S(1)}, bf16[1024,128]{1,0:T(8,128)(2,1)S(1)}, u32[]{:S(2)}, u32[]{:S(2)}) collective-permute-start(bf16[1024,128]{1,0:T(8,128)(2,1)S(1)} %collective-permute-done.refs_0_.refs_8_), channel_id=1, source_target_pairs={{0,1},{1,0},{2,3},{3,2},{4,5},{5,4},{6,7},{7,6},{8,9},{9,8},{10,11... | collective-permute-start | bytes 786440 | tf_op jit(solution)/shard_map/ppermute | solution.py:29
  52.1 3.3 %collective-permute-start.9 = (bf16[384,128]{1,0:T(8,128)(2,1)S(1)}, bf16[384,128]{1,0:T(8,128)(2,1)S(1)}, u32[]{:S(2)}, u32[]{:S(2)}) collective-permute-start(bf16[384,128]{1,0:T(8,128)(2,1)S(1)} %collective-permute-done.8), channel_id=1, source_target_pairs={{0,1},{1,0},{2,3},{3,2},{4,5},{5,4},{6,7},{7,6},{8,9},{9,8},{10,11... | collective-permute-start | bytes 294920 | tf_op jit(solution)/shard_map/ppermute | solution.py:29
  52.5 8.0 %copy-start.5 = (bf16[1024,128]{1,0:T(8,128)(2,1)}, bf16[1024,128]{1,0:T(8,128)(2,1)S(1)}, u32[]{:S(2)}) copy-start(bf16[1024,128]{1,0:T(8,128)(2,1)S(1)} %collective-permute-done.6.refs_2_.refs_14_) | copy-start | bytes 786436
  52.5 7.1 %collective-permute-start.7 = (bf16[1024,128]{1,0:T(8,128)(2,1)S(1)}, bf16[1024,128]{1,0:T(8,128)(2,1)S(1)}, u32[]{:S(2)}, u32[]{:S(2)}) collective-permute-start(bf16[1024,128]{1,0:T(8,128)(2,1)S(1)} %collective-permute-done.6.refs_2_.refs_14_), channel_id=1, source_target_pairs={{0,1},{1,0},{2,3},{3,2},{4,5},{5,4},{6,7},{7,6},{8,9},{9,8},{10,11... | collective-permute-start | bytes 786440 | tf_op jit(solution)/shard_map/ppermute | solution.py:29
  52.7 7.7 %copy-start.7 = (bf16[1024,128]{1,0:T(8,128)(2,1)}, bf16[1024,128]{1,0:T(8,128)(2,1)S(1)}, u32[]{:S(2)}) copy-start(bf16[1024,128]{1,0:T(8,128)(2,1)S(1)} %collective-permute-done.4.refs_0_.refs_12_) | copy-start | bytes 786436
  52.7 6.9 %collective-permute-start.5 = (bf16[1024,128]{1,0:T(8,128)(2,1)S(1)}, bf16[1024,128]{1,0:T(8,128)(2,1)S(1)}, u32[]{:S(2)}, u32[]{:S(2)}) collective-permute-start(bf16[1024,128]{1,0:T(8,128)(2,1)S(1)} %collective-permute-done.4.refs_0_.refs_12_), channel_id=1, source_target_pairs={{0,1},{1,0},{2,3},{3,2},{4,5},{5,4},{6,7},{7,6},{8,9},{9,8},{10,11... | collective-permute-start | bytes 786440 | tf_op jit(solution)/shard_map/ppermute | solution.py:29
  56.2 0.9 copy-start.6
  56.2 0.8 copy-start.8
  59.6 0.9 copy-start.9
  59.6 0.9 copy-start.10

commit v2 on v1

v2 whole, which is shorter than its diff:
```python
import functools
import math

import jax
import jax.numpy as jnp
from jax import lax
from jax.experimental import pallas as pl
from jax.experimental.pallas import tpu as pltpu
from jax.sharding import PartitionSpec as P

BLK = 128
SPAN = 32
LANES = 128
NEG = -1e30
LIMIT = 1e30
LN2 = math.log(2.0)
VMEM_BYTES = 30 * 1024 * 1024
BF16 = jnp.bfloat16
F32 = jnp.float32


def shifted(value, axis, steps):
    count = lax.axis_size(axis)
    leading, last = (max(0, -steps), min(count, count - steps))
    return lax.ppermute(value, axis, [(source, source + steps) for source in range(leading, last)])


def swapped(value):
    return lax.ppermute(value, "rep", [(0, 1), (1, 0)])


def after(*values):
    return lax.optimization_barrier(values)


def dot(left, right, left_dim, right_dim):
    return lax.dot_general(
        left, right, (((left_dim,), (right_dim,)), ((), ())), preferred_element_type=F32
    )


def sublane_sums(values):
    return jnp.sum(values.reshape(-1, 8, values.shape[1]), axis=0)


def one_hot_rows(places, rows_of, count):
    total = jnp.zeros((places.shape[0], 2 * LANES), F32)
    for start in range(0, count, 512):
        hot = jnp.concatenate(
            [
                jnp.where(
                    places
                    == lax.broadcasted_iota(jnp.int32, places.shape, 1) + (start + lane0),
                    1.0,
                    0.0,
                ).astype(BF16)
                for lane0 in range(0, 512, LANES)
            ],
            axis=1,
        )
        total = total + dot(hot, rows_of(start, 512), 1, 0)
    return total.astype(BF16)


def prep_kernel(cfg, offsets, columns_ref, k_ref, v_ref, *refs):
    tok_rows, slot_pad, near = cfg["tok_rows"], cfg["slot_pad"], cfg["near"]
    marks, places, packed, counts = refs[: near + 1], refs[near + 1 : -2], refs[-2], refs[-1]
    seq_index = lax.axis_index("seq")
    head_index = lax.axis_index("head")
    nvert = columns_ref.shape[1]
    nblocks = tok_rows // BLK
    columns = columns_ref[pl.ds(head_index, 1), :]
    wide = jnp.broadcast_to(columns, (8, nvert))
    shifts = [offsets[head_index, place] // BLK for place in range(offsets.shape[1])]

    def ahead_of(start):
        return jnp.sum((columns < start).astype(jnp.int32))

    after = ahead_of((seq_index + 1) * tok_rows)
    for distance in range(cfg["seq_count"]):
        start = (seq_index - distance) * tok_rows
        ahead = ahead_of(start)
        turned = pltpu.roll(wide, lax.rem(nvert - ahead, nvert), 1)
        if distance < near:
            counts[distance] = after - ahead
        after = ahead
        for tile in range(slot_pad // BLK):
            part = slice(tile * BLK, (tile + 1) * BLK)
            listed = jnp.broadcast_to(turned[0:1, part], (BLK, BLK)).T
            inside = (listed >= start) & (listed < start + tok_rows) & (start >= 0)
            lane = lax.broadcasted_iota(jnp.int32, listed.shape, 1)
            gap = seq_index * nblocks + lane - lax.shift_right_arithmetic(listed, 7)
            seen = inside & (gap > 0)
            for shift in shifts:
                seen = seen & (gap != shift)
            where = slice(tile * BLK, (tile + 1) * BLK)
            if distance >= near:
                row0 = (distance - near) * slot_pad + tile * BLK
                where = slice(row0, row0 + BLK)
            marks[min(distance, near)][where, :] = jnp.where(seen, 0.0, NEG).astype(BF16)
            if distance < near:
                places[distance][where, :] = jnp.where(inside, listed - start, -1)
    packed[...] = one_hot_rows(
        places[0][...],
        lambda row0, rows: jnp.concatenate(
            [k_ref[row0 : row0 + rows, :], v_ref[row0 : row0 + rows, :]], axis=1
        ),
        tok_rows,
    )


def prep(offsets, columns, key_rows, value_rows, seq_count, near, slot_pad):
    def whole(shape):
        return pl.BlockSpec(shape, lambda step, offsets: (0, 0))

    far_rows = max(seq_count - near, 1) * slot_pad
    shapes = [(slot_pad, LANES)] * near + [(far_rows, LANES)]
    places = [(slot_pad, LANES)] * near
    return pl.pallas_call(
        functools.partial(
            prep_kernel,
            dict(tok_rows=key_rows.shape[0], slot_pad=slot_pad, near=near, seq_count=seq_count),
        ),
        grid_spec=pltpu.PrefetchScalarGridSpec(
            num_scalar_prefetch=1,
            grid=(1,),
            in_specs=[whole(a.shape) for a in (columns, key_rows, value_rows)],
            out_specs=[whole(shape) for shape in shapes + places + [(slot_pad, 2 * LANES)]]
            + [pl.BlockSpec(memory_space=pltpu.SMEM)],
        ),
        out_shape=[jax.ShapeDtypeStruct(shape, BF16) for shape in shapes]
        + [jax.ShapeDtypeStruct(shape, jnp.int32) for shape in places]
        + [
            jax.ShapeDtypeStruct((slot_pad, 2 * LANES), BF16),
            jax.ShapeDtypeStruct((8,), jnp.int32),
        ],
        compiler_params=pltpu.CompilerParams(vmem_limit_bytes=VMEM_BYTES),
        cost_estimate=pl.CostEstimate(flops=1 << 31, bytes_accessed=1 << 20, transcendentals=0),
        name="prepare",
    )(offsets, columns, key_rows, value_rows)


def stage_kernel(cfg, offsets, counts, q_ref, *refs):
    refs = list(refs)
    nslash = offsets.shape[1]
    heads = q_ref.shape[1] // LANES
    width = heads * BLK
    per_step = cfg["per_step"]
    factor = cfg["factor"]
    first, last = cfg["first"], cfg["last"]
    sources = cfg["sources"]
    step = pl.program_id(0)
    block_from = cfg["step_from"] * per_step + step * per_step
    block0 = lax.axis_index("seq") * cfg["nblocks"]
    core = lax.axis_index("rep")
    head_index = lax.axis_index("head")

    state_refs = [(refs.pop(0), refs.pop(0)) for _ in range(cfg["states"])]
    vert_refs = [[refs.pop(0), refs.pop(0)] for _ in cfg["groups"]]
    source_refs = [(refs.pop(0), refs.pop(0)) for _ in sources]
    spare_refs = [(refs.pop(0), refs.pop(0)) for _ in range(cfg["spares"])]
    out_a, out_b = refs.pop(0), refs.pop(0)
    pack_out = refs.pop(0) if cfg["packs"] and not last else None
    if sources:
        kx, vx, sems = refs.pop(0), refs.pop(0), refs.pop(0)
    if cfg["packs"]:
        pack_ref = refs.pop(0)
    if last:
        redo_k, redo_e, redo_acc, redo_stat, redo_sems = refs

    def source_copies(swap):
        copies = []
        for place, ((row0, rows, fixed), (mine, other)) in enumerate(zip(sources, source_refs)):
            targets = (vx, kx) if swap and not fixed else (kx, vx)
            for which, (ref, target) in enumerate(zip((mine, other), targets)):
                copies.append(
                    pltpu.make_async_copy(
                        ref, target.at[pl.ds(row0, rows), :], sems.at[2 * place + which]
                    )
                )
        return copies

    if sources:

        @pl.when(step == 0)
        def _():
            @pl.when(core == 0)
            def _():
                for copy in source_copies(False):
                    copy.start()

            @pl.when(core != 0)
            def _():
                for copy in source_copies(True):
                    copy.start()

            for copy in source_copies(False):
                copy.wait()
            if cfg["packs"]:
                row0 = cfg["pack_row0"]
                pack_ref[...] = one_hot_rows(
                    vert_refs[0][0][...],
                    lambda at, rows: jnp.concatenate(
                        [
                            kx[row0 + at : row0 + at + rows, :],
                            vx[row0 + at : row0 + at + rows, :],
                        ],
                        axis=1,
                    ),
                    cfg["tok_rows"],
                )
                if pack_out is not None:
                    pack_out[...] = pack_ref[...]

    if cfg["packs"]:
        vert_refs[0][0] = pack_ref

    def tile_rows(index):
        return pl.ds(pl.multiple_of(index * BLK, BLK), BLK)

    def slash_tile(block, place):
        shift = offsets[head_index, place] // BLK
        bias = jnp.where(block0 + block - shift >= 0, 0.0, NEG).astype(F32)
        return jnp.maximum(cfg["own_tile"] + block - shift, 0), bias

    def query_rows(unit):
        rows = slice(unit * BLK, (unit + 1) * BLK)
        return jnp.concatenate(
            [q_ref[rows, h * LANES : (h + 1) * LANES] for h in range(heads)], axis=0
        )

    def marked(query, block):
        lane = lax.broadcasted_iota(jnp.int32, (query.shape[0], LANES), 1)
        return jnp.concatenate([query, jnp.where(lane == block, 1.0, 0.0).astype(BF16)], axis=1)

    def finish(unit, acc, sums, peak):
        total = jnp.sum(sums, axis=0, keepdims=True)
        result = (acc * (1.0 / total)).astype(BF16)
        norm = peak[:1] * LN2 + jnp.log(total)
        for h in range(heads):
            part = slice(h * LANES, (h + 1) * LANES)
            out_a[unit * BLK : (unit + 1) * BLK, part] = result[:, part].T
            out_b[h : h + 1, unit * BLK : (unit + 1) * BLK] = norm[:, part]
        return total

    def one_unit(unit, tiles, with_slash, state):
        block = block_from + unit
        query = query_rows(unit)
        rows = slice(unit * BLK, (unit + 1) * BLK)
        stat = 2 * 8 * unit
        acc = sums = None
        if first:
            own = tile_rows(cfg["own_tile"] + block)
            scores = dot(kx[own, :], query, 1, 1)
            key_at = lax.broadcasted_iota(jnp.int32, scores.shape, 0)
            query_at = lax.broadcasted_iota(jnp.int32, scores.shape, 1) % BLK
            scores = jnp.where(key_at <= query_at, scores, NEG) * factor
            peak = jnp.broadcast_to(jnp.max(scores, axis=0, keepdims=True), (8, width))
            weights = jnp.exp2(scores - peak[:1]).astype(BF16)
            sums = sublane_sums(weights.astype(F32))
            acc = dot(vx[own, :], weights, 0, 0)
        else:
            acc_in, stat_in = state_refs[state]
            sums = stat_in[stat : stat + 8, :]
            peak = stat_in[stat + 8 : stat + 16, :]
        base = peak[:1]
        if sum(tiles):
            keys = jnp.concatenate(
                [
                    jnp.concatenate([kv[: n * BLK, :LANES], mark[: n * BLK, :]], axis=1)
                    for n, (kv, mark) in zip(tiles, vert_refs)
                    if n
                ],
                axis=0,
            )
            values = jnp.concatenate(
                [kv[: n * BLK, LANES:] for n, (kv, _) in zip(tiles, vert_refs) if n], axis=0
            )
            weights = jnp.exp2(dot(keys, marked(query, block), 1, 1) * factor - base).astype(BF16)
            sums = sums + sublane_sums(weights.astype(F32))
            more = dot(values, weights, 0, 0)
            acc = more if acc is None else acc + more
        if with_slash:
            chosen = [slash_tile(block, place) for place in range(1, nslash)]
            keys = jnp.concatenate([kx[tile_rows(index), :] for index, _ in chosen], axis=0)
            values = jnp.concatenate([vx[tile_rows(index), :] for index, _ in chosen], axis=0)
            scores = dot(keys, query, 1, 1)
            parts = []
            for place, (_, bias) in enumerate(chosen):
                weights = jnp.exp2(
                    scores[place * BLK : (place + 1) * BLK, :] * factor + (bias - base)
                ).astype(BF16)
                sums = sums + sublane_sums(weights.astype(F32))
                parts.append(weights)
            more = dot(values, jnp.concatenate(parts, axis=0), 0, 0)
            acc = more if acc is None else acc + more
        if not first:
            acc = acc_in[rows, :] + acc
        if last:
            return finish(unit, acc, sums, peak)
        out_a[rows, :] = acc
        out_b[stat : stat + 8, :] = sums
        out_b[stat + 8 : stat + 16, :] = peak
        return None

    def redo(unit):
        block = block_from + unit
        query = query_rows(unit)
        copies = []
        row0 = 0
        for place, (kv, mark) in enumerate(spare_refs):
            part = pl.ds(row0, kv.shape[0])
            copies.append(pltpu.make_async_copy(kv, redo_k.at[part, :], redo_sems.at[2 * place]))
            copies.append(
                pltpu.make_async_copy(mark, redo_e.at[part, :], redo_sems.at[2 * place + 1])
            )
            row0 += kv.shape[0]
        for copy in copies:
            copy.start()
        for copy in copies:
            copy.wait()
        if cfg["packs"]:
            redo_k[row0 : row0 + pack_ref.shape[0], :] = pack_ref[...]
            redo_e[row0 : row0 + pack_ref.shape[0], :] = vert_refs[0][1][...]
        redo_acc[...] = jnp.zeros_like(redo_acc)
        redo_stat[0:8, :] = jnp.zeros((8, width), F32)
        redo_stat[8:16, :] = jnp.full((8, width), NEG, F32)

        def merge(scores, values):
            peak = redo_stat[8:16, :]
            high = jnp.maximum(peak, jnp.max(scores, axis=0, keepdims=True))
            weights = jnp.where(scores > 1e-3 * NEG, jnp.exp2(scores - high[:1]), 0.0).astype(BF16)
            shrink = jnp.exp2(peak - high)
            redo_stat[0:8, :] = redo_stat[0:8, :] * shrink + sublane_sums(weights.astype(F32))
            redo_stat[8:16, :] = high
            redo_acc[...] = redo_acc[...] * shrink[:1] + dot(values, weights, 0, 0)

        def slash_step(place, carry):
            index, bias = slash_tile(block, place)
            scores = dot(kx[tile_rows(index), :], query, 1, 1) * factor + bias
            key_at = lax.broadcasted_iota(jnp.int32, scores.shape, 0)
            query_at = lax.broadcasted_iota(jnp.int32, scores.shape, 1) % BLK
            reach = jnp.where(offsets[head_index, place] > 0, BLK, 0)
            merge(jnp.where(key_at <= query_at + reach, scores, NEG), vx[tile_rows(index), :])
            return carry

        def vert_step(tile, carry):
            here = tile_rows(tile)
            keys = jnp.concatenate([redo_k[here, :LANES], redo_e[here, :]], axis=1)
            merge(dot(keys, marked(query, block), 1, 1) * factor, redo_k[here, LANES:])
            return carry

        lax.fori_loop(0, nslash, slash_step, 0)
        lax.fori_loop(0, redo_k.shape[0] // BLK, vert_step, 0)
        finish(unit, redo_acc[...], redo_stat[0:8, :], redo_stat[8:16, :])

    def whole_step(tiles, with_slash, state):
        totals = [one_unit(unit, tiles, with_slash, state) for unit in range(per_step)]
        if last:
            worst = jnp.zeros((1, width), F32)
            for total in totals:
                worst = jnp.maximum(worst, jnp.where(total < LIMIT, 0.0, 1.0))

            @pl.when(jnp.max(worst) > 0.0)
            def _():
                for unit in range(per_step):
                    redo(unit)

    def sized_step(with_slash, state):
        groups = cfg["groups"]
        limited = [g for g, n in enumerate(groups) if n > 2 and cfg["counted"][g] is not None]
        if not limited:
            whole_step(groups, with_slash, state)
            return
        fits = functools.reduce(
            jnp.logical_and, [counts[cfg["counted"][g]] <= 2 * BLK for g in limited]
        )

        @pl.when(fits)
        def _():
            few = [2 if g in limited else n for g, n in enumerate(groups)]
            whole_step(few, with_slash, state)

        @pl.when(jnp.logical_not(fits))
        def _():
            whole_step(groups, with_slash, state)

    slash_from, slash_to = cfg["slash_steps"]
    if slash_from >= slash_to:
        sized_step(False, 0)
    elif slash_from <= 0 and slash_to >= cfg["steps"]:
        sized_step(True, 0)
    else:
        within = (step >= slash_from) & (step < slash_to)

        @pl.when(within)
        def _():
            sized_step(True, 0)

        @pl.when(jnp.logical_not(within))
        def _():
            sized_step(False, cfg["states"] - 1)


def stage(
    offsets, counts, queries, states, verts, counted, sources, spare, *,
    blocks, first=False, last=False, slash=(0, 0), own_tile=0, tiles=0, pack_row0=None,
    per_step=4, cost=6,
):
    rows, columns = queries.shape
    heads = columns // LANES
    width = heads * BLK
    step_from = blocks[0] // per_step
    steps = (blocks[1] - blocks[0]) // per_step
    packs = pack_row0 is not None
    cfg = dict(
        per_step=per_step,
        nblocks=rows // BLK,
        tok_rows=rows,
        step_from=step_from,
        steps=steps,
        slash_steps=((slash[0] - blocks[0]) // per_step, (slash[1] - blocks[0]) // per_step),
        factor=1.0 / (math.sqrt(LANES) * LN2),
        first=first,
        last=last,
        states=len(states),
        own_tile=own_tile,
        groups=[mark.shape[0] // BLK for _, mark in verts],
        counted=counted,
        sources=[(row0, mine.shape[0], fixed) for row0, fixed, mine, _ in sources],
        spares=len(spare),
        packs=packs,
        pack_row0=pack_row0,
    )

    def moving(block_rows, from_step=0, count=steps):
        return pl.BlockSpec(
            (block_rows * per_step, width),
            lambda step, *_: (jnp.clip(step - from_step, 0, count - 1), 0),
        )

    def whole(array):
        return pl.BlockSpec(array.shape, lambda step, *_: (0, 0))

    anywhere = pl.BlockSpec(memory_space=pl.ANY)
    operands = [queries]
    specs = [pl.BlockSpec((BLK * per_step, columns), lambda s, *_: (s + step_from, 0))]
    for (array_a, array_b), from_block in states:
        count = array_a.shape[0] // (BLK * per_step)
        operands += [array_a, array_b]
        from_step = from_block // per_step - step_from
        specs += [moving(BLK, from_step, count), moving(16, from_step, count)]
    for pair in verts:
        operands += list(pair)
        specs += [whole(array) for array in pair]
    for _, _, mine, other in sources:
        operands += [mine, other]
        specs += [anywhere, anywhere]
    for pair in spare:
        operands += list(pair)
        specs += [anywhere, anywhere]
    scratch = []
    if sources:
        scratch += [
            pltpu.VMEM((tiles * BLK, LANES), BF16),
            pltpu.VMEM((tiles * BLK, LANES), BF16),
            pltpu.SemaphoreType.DMA((2 * len(sources),)),
        ]
    slot_pad = verts[0][1].shape[0] if verts else 0
    if packs:
        scratch += [pltpu.VMEM((slot_pad, 2 * LANES), BF16)]
    if last:
        out_shape = [
            jax.ShapeDtypeStruct((rows, columns), BF16),
            jax.ShapeDtypeStruct((heads, rows), F32),
        ]
        out_specs = [
            pl.BlockSpec((BLK * per_step, columns), lambda s, *_: (s, 0)),
            pl.BlockSpec((heads, BLK * per_step), lambda s, *_: (0, s)),
        ]
        spare_rows = sum(kv.shape[0] for kv, _ in spare) + slot_pad * packs
        scratch += [
            pltpu.VMEM((spare_rows, 2 * LANES), BF16),
            pltpu.VMEM((spare_rows, LANES), BF16),
            pltpu.VMEM((BLK, width), F32),
            pltpu.VMEM((16, width), F32),
            pltpu.SemaphoreType.DMA((2 * len(spare),)),
        ]
    else:
        out_shape = [
            jax.ShapeDtypeStruct((steps * per_step * BLK, width), F32),
            jax.ShapeDtypeStruct((steps * per_step * 16, width), F32),
        ]
        out_specs = [moving(BLK), moving(16)]
        if packs:
            out_shape.append(jax.ShapeDtypeStruct((slot_pad, 2 * LANES), BF16))
            out_specs.append(pl.BlockSpec((slot_pad, 2 * LANES), lambda s, *_: (0, 0)))
    return pl.pallas_call(
        functools.partial(stage_kernel, cfg),
        grid_spec=pltpu.PrefetchScalarGridSpec(
            num_scalar_prefetch=2,
            grid=(steps,),
            in_specs=specs,
            out_specs=out_specs,
            scratch_shapes=scratch,
        ),
        out_shape=out_shape,
        compiler_params=pltpu.CompilerParams(vmem_limit_bytes=VMEM_BYTES),
        cost_estimate=pl.CostEstimate(
            flops=cost * 1000000000, bytes_accessed=1 << 20, transcendentals=0
        ),
        name="attend_stage",
    )(offsets, counts, *operands)


def body(queries, key_rows, value_rows, vertical_columns, slash_offsets):
    seq_count = lax.axis_size("seq")
    core = lax.axis_index("rep")
    tok_rows = queries.shape[0]
    nblocks = tok_rows // BLK
    radius = (SPAN + nblocks - 2) // nblocks
    slot_count = 3 * vertical_columns.shape[1] // (2 * seq_count)
    slot_pad = -(-slot_count // BLK) * BLK
    near = radius + 1

    payload = jnp.where(core == 0, key_rows, value_rows)
    everything = (0, nblocks)
    moved = shifted(payload, "seq", 1)

    prepared = prep(
        slash_offsets, vertical_columns, key_rows, value_rows, seq_count, near, slot_pad
    )
    marks, places = prepared[: near + 1], prepared[near + 1 : -2]
    own_pack, counts = prepared[-2:]
    run = functools.partial(stage, slash_offsets, counts, queries, blocks=everything)

    own_verts = (own_pack, marks[0])
    own_row0 = radius * tok_rows
    far_moved = []
    if seq_count > near:
        far_payload = jnp.where(core == 0, own_pack[:, :LANES], own_pack[:, LANES:])
        far_moved = [
            shifted(far_payload, "seq", distance) for distance in range(near, seq_count)
        ]
    state = run(
        [], [own_verts], [0], [(0, True, key_rows, value_rows)], [], first=True, tiles=nblocks
    )
    moved, state, far_moved = after(moved, state, far_moved)
    moved2 = shifted(moved, "seq", 1)
    hop1 = (moved, swapped(moved))

    far_verts = []
    if far_moved:
        rows = []
        for mine in far_moved:
            other = swapped(mine)
            rows.append(
                jnp.where(
                    core == 0,
                    jnp.concatenate([mine, other], axis=1),
                    jnp.concatenate([other, mine], axis=1),
                )
            )
        far_verts = [(jnp.concatenate(rows, axis=0) if len(rows) > 1 else rows[0], marks[near])]

    *state, hop_pack = run(
        [(state, 0)], [(places[1], marks[1])] + far_verts, [1] + [None] * len(far_verts),
        [(0, False) + hop1], [], tiles=nblocks, pack_row0=0,
    )
    moved2, state = after(moved2, state)
    return tuple(
        run(
            [(state, 0)], [(places[2], marks[2])], [2],
            [
                (0, False, moved2, swapped(moved2)),
                (own_row0 - tok_rows, False) + hop1,
                (own_row0, True, key_rows, value_rows),
            ],
            [own_verts, (hop_pack, marks[1])] + far_verts,
            last=True, slash=everything, own_tile=radius * nblocks,
            tiles=(radius + 1) * nblocks, pack_row0=0,
        )
    )


def solution(mesh):
    placed = (
        P(("groups", "seq"), ("head", "rep")),
        P(("groups", "seq"), "head"),
        P(("groups", "seq"), "head"),
        P("groups", None),
        P("groups", None),
    )
    return jax.shard_map(
        body,
        mesh=mesh,
        in_specs=placed,
        out_specs=(P(("groups", "seq"), ("head", "rep")), P(("head", "rep"), ("groups", "seq"))),
        check_vma=False,
    )
```

time: 87.5 us -> 55.9 us (0.64)
  other arithmetic: 12.2 us -> 1.18 us
  Pallas kernels: 43.8 us -> 36.1 us
  between operations: 8.56 us -> 0.93 us
  starting transfers between devices: 16.3 us -> 10.1 us
  waiting for transfers between devices: 0.03 us -> 3.72 us
  local copies, waits for them, and re-layouts: 5.71 us -> 3.46 us
    convert_element_type x1 -> x0, other arithmetic: 6.89 us -> none  [marks_of(): return jnp.where(seen, 0.0, NEG).astype(BF16)]
    ppermute x5 -> x3, starting transfers between devices: 15.1 us -> 9.56 us  [shifted(): lax.ppermute(value, axis, [(source, source + steps) for source in range(l...]
    pallas_call x3 -> x1, Pallas kernels: 7.56 us -> 2.32 us  [prep(): pl.pallas_call(functools.partial(prep_kernel, dict(tok_rows=key_rows.shap...]
    unnamed x24 -> x14, local copies, waits for them, and re-layouts: 0.7 us -> 3.46 us
    pallas_call x2 -> x3, Pallas kernels: 36.3 us -> 33.8 us  [stage(): pl.pallas_call(functools.partial(stage_kernel, cfg), grid_spec=pltpu.Pref...]
    broadcast_in_dim x3 -> x0, local copies, waits for them, and re-layouts: 2.46 us -> none  [body(): jnp.broadcast_to(place[:, None], (slot_pad, LANES))]
    ppermute x5 -> x3, waiting for transfers between devices: 0.01 us -> 2.13 us  [swapped(): return lax.ppermute(value, 'rep', [(0, 1), (1, 0)])]
    reduce_sum x3 -> x0, other arithmetic: 2.02 us -> none  [the longest x2 1.3 us: body(): counts = [jnp.sum(valid.astype(jnp.int32)) for _, valid, _ in near]]
  transfers between devices with their start and end apart: 10 -> 6, of which waited for: 0 -> 3; matrix products, arithmetic and copies ran while one was open for 16% -> 0% of each run, Pallas kernels for 17% -> 38%
where the time goes in v2:
time: 55.9 us; the launch traced here: 55.5 us
  Pallas kernels  36.1 us (65%)
  starting transfers between devices  10.1 us (18%)
  waiting for transfers between devices  3.72 us (7%)
  local copies, waits for them, and re-layouts  3.46 us (6%)
  other arithmetic  1.18 us (2%)
  between operations  0.93 us (2%)
    pallas_call x3, Pallas kernels, stage(): pl.pallas_call(functools.partial(stage_kernel, cfg), grid_spec=pltpu.Pref...  33.8 us
    ppermute x3, starting transfers between devices, shifted(): lax.ppermute(value, axis, [(source, source + steps) for source in range(l...  9.56 us
    unnamed x14, local copies, waits for them, and re-layouts  3.46 us
    pallas_call x1, Pallas kernels, prep(): pl.pallas_call(functools.partial(prep_kernel, dict(tok_rows=key_rows.shap...  2.32 us
    ppermute x3, waiting for transfers between devices, swapped(): return lax.ppermute(value, 'rep', [(0, 1), (1, 0)])  2.13 us
    ppermute x3, waiting for transfers between devices, shifted(): lax.ppermute(value, axis, [(source, source + steps) for source in range(l...  1.58 us
  transfers between devices with their start and end apart: 6, of which 3 were waited for; matrix products, arithmetic and copies ran while one was open for 0% of the time, Pallas kernels for 38%

profile of v2, /device:TPU:0, one launch (start us, length us, event | category | flops | bytes accessed | tf_op | source)
XLA Modules:
  0.0 55.5 jit_solution(309812576307279884)
XLA Ops:
  0.6 1.1 %broadcast_select_fusion = bf16[2048,128]{1,0:T(8,128)(2,1)S(1)} fusion(bf16[2048,128]{1,0:T(8,128)(2,1)} %refs_8_.1, bf16[2048,128]{1,0:T(8,128)(2,1)} %refs_9_.1, pred[]{:T(512)S(6)} %eq.2), kind=kLoop, calls=%fused_computation | loop fusion | flops 262144 | bytes 1572865 | tf_op jit(solution)/shard_map/jit(_where)/select_n | solution.py:526
  1.7 5.0 %collective-permute-start = (bf16[2048,128]{1,0:T(8,128)(2,1)S(1)}, bf16[2048,128]{1,0:T(8,128)(2,1)S(1)}, u32[]{:S(2)}, u32[]{:S(2)}) collective-permute-start(bf16[2048,128]{1,0:T(8,128)(2,1)S(1)} %broadcast_select_fusion), channel_id=1, source_target_pairs={{0,4},{4,8},{8,12},{1,5},{5,9},{9,13},{2,6},{6,10},{10,14},{3,7},{... | collective-permute-start | bytes 1572872 | tf_op jit(solution)/shard_map/ppermute | solution.py:25
  6.7 0.0 copy-start
  6.7 1.0 %copy-done = bf16[2048,128]{1,0:T(8,128)(2,1)S(1)} copy-done((bf16[2048,128]{1,0:T(8,128)(2,1)S(1)}, bf16[2048,128]{1,0:T(8,128)(2,1)}, u32[]{:S(2)}) %copy-start) | copy-done | bytes 524312
  7.8 0.0 copy-start.2
  7.8 1.0 %copy-done.2 = bf16[2048,128]{1,0:T(8,128)(2,1)S(1)} copy-done((bf16[2048,128]{1,0:T(8,128)(2,1)S(1)}, bf16[2048,128]{1,0:T(8,128)(2,1)}, u32[]{:S(2)}) %copy-start.2) | copy-done | bytes 524312
  8.8 0.0 copy-start.5
  8.8 0.7 %copy-done.5 = s32[2,1024]{1,0:T(2,128)S(1)} copy-done((s32[2,1024]{1,0:T(2,128)S(1)}, s32[2,1024]{1,0:T(2,128)}, u32[]{:S(2)}) %copy-start.5) | copy-done | bytes 8216
  9.5 0.0 copy-start.6
  9.5 0.7 %copy-done.6 = s32[2,8]{1,0:T(2,128)S(1)} copy-done((s32[2,8]{1,0:T(2,128)S(1)}, s32[2,8]{1,0:T(2,128)}, u32[]{:S(2)}) %copy-start.6) | copy-done | bytes 88
  10.2 0.0 copy-start.1
  10.2 0.0 copy-start.3
  10.2 0.0 copy-start.4
  10.2 2.3 %prepare.1 = (bf16[384,128]{1,0:T(8,128)(2,1)S(1)}, bf16[384,128]{1,0:T(8,128)(2,1)S(1)}, bf16[384,128]{1,0:T(8,128)(2,1)S(1)}, bf16[384,128]{1,0:T(8,128)(2,1)S...) custom-call(s32[2,8]{1,0:T(2,128)S(1)} %copy-done.6, ...), custom_call_target="tpu_custom_call" | custom-call | flops 2147483648 | bytes 1048576 | tf_op jit(solution)/shard_map/prepare/pallas_call | solution.py:119
  12.5 3.3 %collective-permute-start.1 = (bf16[384,128]{1,0:T(8,128)(2,1)S(1)}, bf16[384,128]{1,0:T(8,128)(2,1)S(1)}, u32[]{:S(2)}, u32[]{:S(2)}) collective-permute-start(bf16[384,128]{1,0:T(8,128)(2,1)S(1)} %slice_select_fusion), channel_id=1, source_target_pairs={{0,12},{1,13},{2,14},{3,15},{16,28},{17,29},{18,30},{19,31}} | collective-permute-start | bytes 294920 | tf_op jit(solution)/shard_map/ppermute | solution.py:25
  15.8 0.0 copy-done.1
  15.8 0.0 copy-done.3
  15.9 0.0 copy-done.4
  15.9 8.9 %attend_stage.3 = (f32[2048,512]{1,0:T(8,128)S(1)}, f32[256,512]{1,0:T(8,128)S(1)}) custom-call(s32[2,8]{1,0:T(2,128)S(1)} %copy-done.6, s32[8]{0:T(128)S(1)} %get-tuple-element.22.counts, bf16[2048,512]{1,0:T(8,128)(2,1)S(1)} %copy-done.4, bf16[384,256]{1,0:T(8,128)(2,1)S(1)} %get-tuple-element.23.refs_0_.refs_10_, ...), custom_call_target="tpu_custom_call" | custom-call | flops 6000000000 | bytes 1048576 | tf_op jit(solution)/shard_map/attend_stage/pallas_call | solution.py:498
  24.8 0.0 collective-permute-done.1
  24.8 0.0 collective-permute-done.refs_6_
  24.8 0.1 collective-permute-start.4
  24.9 0.5 collective-permute-start.3
  25.4 1.3 %collective-permute-start.2 = (bf16[2048,128]{1,0:T(8,128)(2,1)S(1)}, bf16[2048,128]{1,0:T(8,128)(2,1)S(1)}, u32[]{:S(2)}, u32[]{:S(2)}) collective-permute-start(bf16[2048,128]{1,0:T(8,128)(2,1)S(1)} %collective-permute-done.refs_6_), channel_id=1, source_target_pairs={{0,4},{4,8},{8,12},{1,5},{5,9},{9,13},{2,6},{6,10},{10,14},{3,7},{... | collective-permute-start | bytes 1572872 | tf_op jit(solution)/shard_map/ppermute | solution.py:25
  26.7 0.2 collective-permute-done.3
  26.9 0.1 maximum_select_fusion.refs_4_.refs_14_
  27.0 0.0 collective-permute-done.4.refs_7_
  27.0 9.8 %attend_stage.4 = (f32[2048,512]{1,0:T(8,128)S(1)}, f32[256,512]{1,0:T(8,128)S(1)}, bf16[384,256]{1,0:T(8,128)(2,1)S(1)}) custom-call(s32[2,8]{1,0:T(2,128)S(1)} %copy-done.6, s32[8]{0:T(128)S(1)} %get-tuple-element.22.counts, bf16[2048,512]{1,0:T(8,128)(2,1)S(1)} %copy-done.4, f32[2048,512]{1,0:T(8,128)S(1)} %get-tuple-element.28.refs_0_, ...), custom_call_target="tpu_custom_call" | custom-call | flops 6000000000 | bytes 1048576 | tf_op jit(solution)/shard_map/attend_stage/pallas_call | solution.py:498
  36.8 1.6 %collective-permute-done.2.refs_4_ = bf16[2048,128]{1,0:T(8,128)(2,1)S(1)} collective-permute-done((bf16[2048,128]{1,0:T(8,128)(2,1)S(1)}, bf16[2048,128]{1,0:T(8,128)(2,1)S(1)}, u32[]{:S(2)}, u32[]{:S(2)}) %collective-permute-start.2) | collective-permute-done | bytes 524320 | tf_op jit(solution)/shard_map/ppermute | solution.py:25
  38.3 0.0 collective-permute-start.5
  38.4 1.9 %collective-permute-done.5.refs_5_ = bf16[2048,128]{1,0:T(8,128)(2,1)S(1)} collective-permute-done((bf16[2048,128]{1,0:T(8,128)(2,1)S(1)}, bf16[2048,128]{1,0:T(8,128)(2,1)S(1)}, u32[]{:S(2)}, u32[]{:S(2)}) %collective-permute-start.5) | collective-permute-done | bytes 524320 | tf_op jit(solution)/shard_map/ppermute | solution.py:29
  40.3 15.1 %attend_stage.5 = (bf16[2048,512]{1,0:T(8,128)(2,1)}, f32[4,2048]{1,0:T(4,128)}) custom-call(s32[2,8]{1,0:T(2,128)S(1)} %copy-done.6, s32[8]{0:T(128)S(1)} %get-tuple-element.22.counts, bf16[2048,512]{1,0:T(8,128)(2,1)S(1)} %copy-done.4, f32[2048,512]{1,0:T(8,128)S(1)} %get-tuple-element.36.refs_0_, f32[256,512]{1,0:T(8,128)S(1)} %get-tuple-element.37.refs_1_, ...), custom_call_target="tpu_custom_call" | custom-call | flops 6000000000 | bytes 1048576 | tf_op jit(solution)/shard_map/attend_stage/pallas_call | solution.py:498
  (1 shorter events, 0.0 us)
Async XLA Ops:
  1.7 23.0 %collective-permute-start = (bf16[2048,128]{1,0:T(8,128)(2,1)S(1)}, bf16[2048,128]{1,0:T(8,128)(2,1)S(1)}, u32[]{:S(2)}, u32[]{:S(2)}) collective-permute-start(bf16[2048,128]{1,0:T(8,128)(2,1)S(1)} %broadcast_select_fusion), channel_id=1, source_target_pairs={{0,4},{4,8},{8,12},{1,5},{5,9},{9,13},{2,6},{6,10},{10,14},{3,7},{... | collective-permute-start | bytes 1572872 | tf_op jit(solution)/shard_map/ppermute | solution.py:25
  6.7 1.0 %copy-start = (bf16[2048,128]{1,0:T(8,128)(2,1)S(1)}, bf16[2048,128]{1,0:T(8,128)(2,1)}, u32[]{:S(2)}) copy-start(bf16[2048,128]{1,0:T(8,128)(2,1)} %refs_8_.1) | copy-start | bytes 1572868
  7.8 1.0 %copy-start.2 = (bf16[2048,128]{1,0:T(8,128)(2,1)S(1)}, bf16[2048,128]{1,0:T(8,128)(2,1)}, u32[]{:S(2)}) copy-start(bf16[2048,128]{1,0:T(8,128)(2,1)} %refs_9_.1) | copy-start | bytes 1572868
  8.8 0.7 %copy-start.5 = (s32[2,1024]{1,0:T(2,128)S(1)}, s32[2,1024]{1,0:T(2,128)}, u32[]{:S(2)}) copy-start(s32[2,1024]{1,0:T(2,128)} %columns_ref.1) | copy-start | bytes 24580
  9.5 0.7 %copy-start.6 = (s32[2,8]{1,0:T(2,128)S(1)}, s32[2,8]{1,0:T(2,128)}, u32[]{:S(2)}) copy-start(s32[2,8]{1,0:T(2,128)} %offsets.7) | copy-start | bytes 196
  10.2 5.7 %copy-start.1 = (bf16[2048,128]{1,0:T(8,128)(2,1)S(1)}, bf16[2048,128]{1,0:T(8,128)(2,1)}, u32[]{:S(2)}) copy-start(bf16[2048,128]{1,0:T(8,128)(2,1)} %refs_8_.1) | copy-start | bytes 1572868
  10.2 5.7 %copy-start.3 = (bf16[2048,128]{1,0:T(8,128)(2,1)S(1)}, bf16[2048,128]{1,0:T(8,128)(2,1)}, u32[]{:S(2)}) copy-start(bf16[2048,128]{1,0:T(8,128)(2,1)} %refs_9_.1) | copy-start | bytes 1572868
  10.2 5.7 %copy-start.4 = (bf16[2048,512]{1,0:T(8,128)(2,1)S(1)}, bf16[2048,512]{1,0:T(8,128)(2,1)}, u32[]{:S(2)}) copy-start(bf16[2048,512]{1,0:T(8,128)(2,1)} %q_ref.5) | copy-start | bytes 6291460
  12.5 12.2 %collective-permute-start.1 = (bf16[384,128]{1,0:T(8,128)(2,1)S(1)}, bf16[384,128]{1,0:T(8,128)(2,1)S(1)}, u32[]{:S(2)}, u32[]{:S(2)}) collective-permute-start(bf16[384,128]{1,0:T(8,128)(2,1)S(1)} %slice_select_fusion), channel_id=1, source_target_pairs={{0,12},{1,13},{2,14},{3,15},{16,28},{17,29},{18,30},{19,31}} | collective-permute-start | bytes 294920 | tf_op jit(solution)/shard_map/ppermute | solution.py:25
  24.8 2.2 %collective-permute-start.4 = (bf16[2048,128]{1,0:T(8,128)(2,1)S(1)}, bf16[2048,128]{1,0:T(8,128)(2,1)S(1)}, u32[]{:S(2)}, u32[]{:S(2)}) collective-permute-start(bf16[2048,128]{1,0:T(8,128)(2,1)S(1)} %collective-permute-done.refs_6_), channel_id=1, source_target_pairs={{0,1},{1,0},{2,3},{3,2},{4,5},{5,4},{6,7},{7,6},{8,9},{9,8},{10,11... | collective-permute-start | bytes 1572872 | tf_op jit(solution)/shard_map/ppermute | solution.py:29
  24.9 2.0 %collective-permute-start.3 = (bf16[384,128]{1,0:T(8,128)(2,1)S(1)}, bf16[384,128]{1,0:T(8,128)(2,1)S(1)}, u32[]{:S(2)}, u32[]{:S(2)}) collective-permute-start(bf16[384,128]{1,0:T(8,128)(2,1)S(1)} %collective-permute-done.1), channel_id=1, source_target_pairs={{0,1},{1,0},{2,3},{3,2},{4,5},{5,4},{6,7},{7,6},{8,9},{9,8},{10,11... | collective-permute-start | bytes 294920 | tf_op jit(solution)/shard_map/ppermute | solution.py:29
  25.4 13.0 %collective-permute-start.2 = (bf16[2048,128]{1,0:T(8,128)(2,1)S(1)}, bf16[2048,128]{1,0:T(8,128)(2,1)S(1)}, u32[]{:S(2)}, u32[]{:S(2)}) collective-permute-start(bf16[2048,128]{1,0:T(8,128)(2,1)S(1)} %collective-permute-done.refs_6_), channel_id=1, source_target_pairs={{0,4},{4,8},{8,12},{1,5},{5,9},{9,13},{2,6},{6,10},{10,14},{3,7},{... | collective-permute-start | bytes 1572872 | tf_op jit(solution)/shard_map/ppermute | solution.py:25
  38.3 1.9 %collective-permute-start.5 = (bf16[2048,128]{1,0:T(8,128)(2,1)S(1)}, bf16[2048,128]{1,0:T(8,128)(2,1)S(1)}, u32[]{:S(2)}, u32[]{:S(2)}) collective-permute-start(bf16[2048,128]{1,0:T(8,128)(2,1)S(1)} %collective-permute-done.2.refs_4_), channel_id=1, source_target_pairs={{0,1},{1,0},{2,3},{3,2},{4,5},{5,4},{6,7},{7,6},{8,9},{9,8},{10,11... | collective-permute-start | bytes 1572872 | tf_op jit(solution)/shard_map/ppermute | solution.py:29

commit v3 on v2

--- a/solution.py
+++ b/solution.py
@@ -13,6 +13,7 @@
 LANES = 128
 NEG = -1e30
 LIMIT = 1e30
+EARLY = (2, 3)
 LN2 = math.log(2.0)
 VMEM_BYTES = 30 * 1024 * 1024
 BF16 = jnp.bfloat16
@@ -62,13 +63,23 @@
     return total.astype(BF16)
 
 
-def prep_kernel(cfg, offsets, columns_ref, k_ref, v_ref, *refs):
+def prep_kernel(cfg, offsets, columns_hbm, k_hbm, v_hbm, *refs):
+    *refs, columns_ref, k_ref, v_ref, sems = refs
+    moves = [
+        pltpu.make_async_copy(source, target, sems.at[place])
+        for place, (source, target) in enumerate(
+            ((columns_hbm, columns_ref), (k_hbm, k_ref), (v_hbm, v_ref))
+        )
+    ]
+    for move in moves:
+        move.start()
     tok_rows, slot_pad, near = cfg["tok_rows"], cfg["slot_pad"], cfg["near"]
     marks, places, packed, counts = refs[: near + 1], refs[near + 1 : -2], refs[-2], refs[-1]
     seq_index = lax.axis_index("seq")
     head_index = lax.axis_index("head")
     nvert = columns_ref.shape[1]
     nblocks = tok_rows // BLK
+    moves[0].wait()
     columns = columns_ref[pl.ds(head_index, 1), :]
     wide = jnp.broadcast_to(columns, (8, nvert))
     shifts = [offsets[head_index, place] // BLK for place in range(offsets.shape[1])]
@@ -100,6 +111,8 @@
             marks[min(distance, near)][where, :] = jnp.where(seen, 0.0, NEG).astype(BF16)
             if distance < near:
                 places[distance][where, :] = jnp.where(inside, listed - start, -1)
+    moves[1].wait()
+    moves[2].wait()
     packed[...] = one_hot_rows(
         places[0][...],
         lambda row0, rows: jnp.concatenate(
@@ -124,9 +137,15 @@
         grid_spec=pltpu.PrefetchScalarGridSpec(
             num_scalar_prefetch=1,
             grid=(1,),
-            in_specs=[whole(a.shape) for a in (columns, key_rows, value_rows)],
+            in_specs=[pl.BlockSpec(memory_space=pltpu.HBM)] * 3,
             out_specs=[whole(shape) for shape in shapes + places + [(slot_pad, 2 * LANES)]]
             + [pl.BlockSpec(memory_space=pltpu.SMEM)],
+            scratch_shapes=[
+                pltpu.VMEM(columns.shape, jnp.int32),
+                pltpu.VMEM(key_rows.shape, BF16),
+                pltpu.VMEM(value_rows.shape, BF16),
+                pltpu.SemaphoreType.DMA((3,)),
+            ],
         ),
         out_shape=[jax.ShapeDtypeStruct(shape, BF16) for shape in shapes]
         + [jax.ShapeDtypeStruct(shape, jnp.int32) for shape in places]
@@ -166,7 +185,7 @@
     if cfg["packs"]:
         pack_ref = refs.pop(0)
     if last:
-        redo_k, redo_e, redo_acc, redo_stat, redo_sems = refs
+        redo_k, redo_e, redo_acc, redo_stat, redo_sems, redo_flag = refs
 
     def source_copies(swap):
         copies = []
@@ -194,7 +213,8 @@
                 for copy in source_copies(True):
                     copy.start()
 
-            for copy in source_copies(False):
+            waits = source_copies(False)
+            for copy in waits[:2]:
                 copy.wait()
             if cfg["packs"]:
                 row0 = cfg["pack_row0"]
@@ -211,6 +231,8 @@
                 )
                 if pack_out is not None:
                     pack_out[...] = pack_ref[...]
+            for copy in waits[2:]:
+                copy.wait()
 
     if cfg["packs"]:
         vert_refs[0][0] = pack_ref
@@ -223,8 +245,12 @@
         bias = jnp.where(block0 + block - shift >= 0, 0.0, NEG).astype(F32)
         return jnp.maximum(cfg["own_tile"] + block - shift, 0), bias
 
+    def span(unit):
+        start = unit * BLK
+        return pl.ds(start if isinstance(unit, int) else pl.multiple_of(start, BLK), BLK)
+
     def query_rows(unit):
-        rows = slice(unit * BLK, (unit + 1) * BLK)
+        rows = span(unit)
         return jnp.concatenate(
             [q_ref[rows, h * LANES : (h + 1) * LANES] for h in range(heads)], axis=0
         )
@@ -239,11 +265,11 @@
         norm = peak[:1] * LN2 + jnp.log(total)
         for h in range(heads):
             part = slice(h * LANES, (h + 1) * LANES)
-            out_a[unit * BLK : (unit + 1) * BLK, part] = result[:, part].T
-            out_b[h : h + 1, unit * BLK : (unit + 1) * BLK] = norm[:, part]
+            out_a[span(unit), part] = result[:, part].T
+            out_b[h : h + 1, span(unit)] = norm[:, part]
         return total
 
-    def one_unit(unit, tiles, with_slash, state):
+    def one_unit(unit, tiles, chosen_places):
         block = block_from + unit
         query = query_rows(unit)
         rows = slice(unit * BLK, (unit + 1) * BLK)
@@ -260,7 +286,7 @@
             sums = sublane_sums(weights.astype(F32))
             acc = dot(vx[own, :], weights, 0, 0)
         else:
-            acc_in, stat_in = state_refs[state]
+            acc_in, stat_in = state_refs[0]
             sums = stat_in[stat : stat + 8, :]
             peak = stat_in[stat + 8 : stat + 16, :]
         base = peak[:1]
@@ -280,8 +306,8 @@
             sums = sums + sublane_sums(weights.astype(F32))
             more = dot(values, weights, 0, 0)
             acc = more if acc is None else acc + more
-        if with_slash:
-            chosen = [slash_tile(block, place) for place in range(1, nslash)]
+        if chosen_places:
+            chosen = [slash_tile(block, place) for place in chosen_places]
             keys = jnp.concatenate([kx[tile_rows(index), :] for index, _ in chosen], axis=0)
             values = jnp.concatenate([vx[tile_rows(index), :] for index, _ in chosen], axis=0)
             scores = dot(keys, query, 1, 1)
@@ -354,57 +380,60 @@
         lax.fori_loop(0, redo_k.shape[0] // BLK, vert_step, 0)
         finish(unit, redo_acc[...], redo_stat[0:8, :], redo_stat[8:16, :])
 
-    def whole_step(tiles, with_slash, state):
-        totals = [one_unit(unit, tiles, with_slash, state) for unit in range(per_step)]
+    def redo_one(unit, carry):
+        redo(unit)
+        return carry
+
+    def whole_step(tiles, chosen_places):
+        totals = [one_unit(unit, tiles, chosen_places) for unit in range(per_step)]
         if last:
             worst = jnp.zeros((1, width), F32)
             for total in totals:
                 worst = jnp.maximum(worst, jnp.where(total < LIMIT, 0.0, 1.0))
-
-            @pl.when(jnp.max(worst) > 0.0)
+            redo_flag[0] = jnp.where(jnp.max(worst) > 0.0, 1, 0)
+
+    groups = cfg["groups"]
+    limited = [g for g, n in enumerate(groups) if n > 2 and cfg["counted"][g] is not None]
+    few = [2 if g in limited else n for g, n in enumerate(groups)]
+    fits = functools.reduce(
+        jnp.logical_and, [counts[cfg["counted"][g]] <= 2 * BLK for g in limited], step >= 0
+    )
+    every = list(range(1, nslash))
+
+    def sized_step(wanted, places):
+        if limited:
+
+            @pl.when(jnp.logical_and(fits, wanted))
             def _():
-                for unit in range(per_step):
-                    redo(unit)
-
-    def sized_step(with_slash, state):
-        groups = cfg["groups"]
-        limited = [g for g, n in enumerate(groups) if n > 2 and cfg["counted"][g] is not None]
-        if not limited:
-            whole_step(groups, with_slash, state)
-            return
-        fits = functools.reduce(
-            jnp.logical_and, [counts[cfg["counted"][g]] <= 2 * BLK for g in limited]
-        )
-
-        @pl.when(fits)
+                whole_step(few, places)
+
+        @pl.when(jnp.logical_and(jnp.logical_not(fits), wanted) if limited else wanted)
         def _():
-            few = [2 if g in limited else n for g, n in enumerate(groups)]
-            whole_step(few, with_slash, state)
-
-        @pl.when(jnp.logical_not(fits))
+            whole_step(groups, places)
+
+    if not cfg["ahead"]:
+        sized_step(step >= 0, [])
+        return
+    share = cfg["steps"] // len(cfg["ahead"])
+    for part, ahead in enumerate(cfg["ahead"]):
+        within = (step >= part * share) & (step < (part + 1) * share)
+        early = offsets[head_index, ahead] <= cfg["tok_rows"] + part * share * per_step * BLK
+        sized_step(jnp.logical_and(within, early), every[ahead:] if last else every[:ahead])
+
+        @pl.when(jnp.logical_and(within, jnp.logical_not(early)))
         def _():
-            whole_step(groups, with_slash, state)
-
-    slash_from, slash_to = cfg["slash_steps"]
-    if slash_from >= slash_to:
-        sized_step(False, 0)
-    elif slash_from <= 0 and slash_to >= cfg["steps"]:
-        sized_step(True, 0)
-    else:
-        within = (step >= slash_from) & (step < slash_to)
-
-        @pl.when(within)
+            whole_step(groups, every if last else [])
+
+    if last:
+
+        @pl.when(redo_flag[0] > 0)
         def _():
-            sized_step(True, 0)
-
-        @pl.when(jnp.logical_not(within))
-        def _():
-            sized_step(False, cfg["states"] - 1)
+            lax.fori_loop(0, per_step, redo_one, 0)
 
 
 def stage(
     offsets, counts, queries, states, verts, counted, sources, spare, *,
-    blocks, first=False, last=False, slash=(0, 0), own_tile=0, tiles=0, pack_row0=None,
+    blocks, first=False, last=False, ahead=(), own_tile=0, tiles=0, pack_row0=None,
     per_step=4, cost=6,
 ):
     rows, columns = queries.shape
@@ -419,7 +448,7 @@
         tok_rows=rows,
         step_from=step_from,
         steps=steps,
-        slash_steps=((slash[0] - blocks[0]) // per_step, (slash[1] - blocks[0]) // per_step),
+        ahead=ahead,
         factor=1.0 / (math.sqrt(LANES) * LN2),
         first=first,
         last=last,
@@ -485,6 +514,7 @@
             pltpu.VMEM((BLK, width), F32),
             pltpu.VMEM((16, width), F32),
             pltpu.SemaphoreType.DMA((2 * len(spare),)),
+            pltpu.SMEM((1,), jnp.int32),
         ]
     else:
         out_shape = [
@@ -565,7 +595,8 @@
 
     *state, hop_pack = run(
         [(state, 0)], [(places[1], marks[1])] + far_verts, [1] + [None] * len(far_verts),
-        [(0, False) + hop1], [], tiles=nblocks, pack_row0=0,
+        [(0, False) + hop1, (tok_rows, True, key_rows, value_rows)], [], ahead=EARLY,
+        own_tile=nblocks, tiles=2 * nblocks, pack_row0=0,
     )
     moved2, state = after(moved2, state)
     return tuple(
@@ -577,7 +608,7 @@
                 (own_row0, True, key_rows, value_rows),
             ],
             [own_verts, (hop_pack, marks[1])] + far_verts,
-            last=True, slash=everything, own_tile=radius * nblocks,
+            last=True, ahead=EARLY, own_tile=radius * nblocks,
             tiles=(radius + 1) * nblocks, pack_row0=0,
         )
     )

time: 55.9 us -> 55.4 us (level)
  waiting for transfers between devices: 3.72 us -> 2 us
  Pallas kernels: 36.1 us -> 37 us
    ppermute x3, waiting for transfers between devices: 1.58 us -> 0.01 us  [shifted(): lax.ppermute(value, axis, [(source, source + steps) for source in range(l...]
    pallas_call x3, Pallas kernels: 33.8 us -> 34.7 us  [stage(): pl.pallas_call(functools.partial(stage_kernel, cfg), grid_spec=pltpu.Pref...]
  transfers between devices with their start and end apart: 6 -> 6, of which waited for: 3 -> 2; matrix products, arithmetic and copies ran while one was open for 0% -> 0% of each run, Pallas kernels for 38% -> 44%
where the time goes in v3:
time: 55.4 us; the launch traced here: 55 us
  Pallas kernels  37 us (67%)
  starting transfers between devices  10.3 us (19%)
  local copies, waits for them, and re-layouts  3.46 us (6%)
  waiting for transfers between devices  2 us (4%)
  other arithmetic  1.18 us (2%)
  between operations  0.96 us (2%)
    pallas_call x3, Pallas kernels, stage(): pl.pallas_call(functools.partial(stage_kernel, cfg), grid_spec=pltpu.Pref...  34.7 us
    ppermute x3, starting transfers between devices, shifted(): lax.ppermute(value, axis, [(source, source + steps) for source in range(l...  9.56 us
    unnamed x14, local copies, waits for them, and re-layouts  3.46 us
    pallas_call x1, Pallas kernels, prep(): pl.pallas_call(functools.partial(prep_kernel, dict(tok_rows=key_rows.shap...  2.3 us
    ppermute x3, waiting for transfers between devices, swapped(): return lax.ppermute(value, 'rep', [(0, 1), (1, 0)])  1.99 us
  transfers between devices with their start and end apart: 6, of which 2 were waited for; matrix products, arithmetic and copies ran while one was open for 0% of the time, Pallas kernels for 44%

profile of v3, /device:TPU:0, one launch (start us, length us, event | category | flops | bytes accessed | tf_op | source)
XLA Modules:
  0.0 55.0 jit_solution(14893774041683830893)
XLA Ops:
  0.6 1.1 %broadcast_select_fusion = bf16[2048,128]{1,0:T(8,128)(2,1)S(1)} fusion(bf16[2048,128]{1,0:T(8,128)(2,1)} %refs_8_.3, bf16[2048,128]{1,0:T(8,128)(2,1)} %refs_9_.3, pred[]{:T(512)S(6)} %eq.2), kind=kLoop, calls=%fused_computation | loop fusion | flops 262144 | bytes 1572865 | tf_op jit(solution)/shard_map/jit(_where)/select_n | solution.py:556
  1.7 5.0 %collective-permute-start = (bf16[2048,128]{1,0:T(8,128)(2,1)S(1)}, bf16[2048,128]{1,0:T(8,128)(2,1)S(1)}, u32[]{:S(2)}, u32[]{:S(2)}) collective-permute-start(bf16[2048,128]{1,0:T(8,128)(2,1)S(1)} %broadcast_select_fusion), channel_id=1, source_target_pairs={{0,4},{4,8},{8,12},{1,5},{5,9},{9,13},{2,6},{6,10},{10,14},{3,7},{... | collective-permute-start | bytes 1572872 | tf_op jit(solution)/shard_map/ppermute | solution.py:26
  6.7 0.0 copy-start
  6.7 1.0 %copy-done = bf16[2048,128]{1,0:T(8,128)(2,1)S(1)} copy-done((bf16[2048,128]{1,0:T(8,128)(2,1)S(1)}, bf16[2048,128]{1,0:T(8,128)(2,1)}, u32[]{:S(2)}) %copy-start) | copy-done | bytes 524312
  7.8 0.0 copy-start.2
  7.8 1.0 %copy-done.2 = bf16[2048,128]{1,0:T(8,128)(2,1)S(1)} copy-done((bf16[2048,128]{1,0:T(8,128)(2,1)S(1)}, bf16[2048,128]{1,0:T(8,128)(2,1)}, u32[]{:S(2)}) %copy-start.2) | copy-done | bytes 524312
  8.8 0.0 copy-start.5
  8.8 0.7 %copy-done.5 = s32[2,1024]{1,0:T(2,128)S(1)} copy-done((s32[2,1024]{1,0:T(2,128)S(1)}, s32[2,1024]{1,0:T(2,128)}, u32[]{:S(2)}) %copy-start.5) | copy-done | bytes 8216
  9.5 0.0 copy-start.6
  9.5 0.7 %copy-done.6 = s32[2,8]{1,0:T(2,128)S(1)} copy-done((s32[2,8]{1,0:T(2,128)S(1)}, s32[2,8]{1,0:T(2,128)}, u32[]{:S(2)}) %copy-start.6) | copy-done | bytes 88
  10.2 0.0 copy-start.1
  10.2 0.0 copy-start.3
  10.2 0.0 copy-start.4
  10.2 2.3 %prepare.1 = (bf16[384,128]{1,0:T(8,128)(2,1)S(1)}, bf16[384,128]{1,0:T(8,128)(2,1)S(1)}, bf16[384,128]{1,0:T(8,128)(2,1)S(1)}, bf16[384,128]{1,0:T(8,128)(2,1)S...) custom-call(s32[2,8]{1,0:T(2,128)S(1)} %copy-done.6, ...), custom_call_target="tpu_custom_call" | custom-call | flops 2147483648 | bytes 1048576 | tf_op jit(solution)/shard_map/prepare/pallas_call | solution.py:132
  12.5 3.3 %collective-permute-start.1 = (bf16[384,128]{1,0:T(8,128)(2,1)S(1)}, bf16[384,128]{1,0:T(8,128)(2,1)S(1)}, u32[]{:S(2)}, u32[]{:S(2)}) collective-permute-start(bf16[384,128]{1,0:T(8,128)(2,1)S(1)} %slice_select_fusion), channel_id=1, source_target_pairs={{0,12},{1,13},{2,14},{3,15},{16,28},{17,29},{18,30},{19,31}} | collective-permute-start | bytes 294920 | tf_op jit(solution)/shard_map/ppermute | solution.py:26
  15.8 0.0 copy-done.1
  15.8 0.0 copy-done.3
  15.8 0.0 copy-done.4
  15.8 8.9 %attend_stage.3 = (f32[2048,512]{1,0:T(8,128)S(1)}, f32[256,512]{1,0:T(8,128)S(1)}) custom-call(s32[2,8]{1,0:T(2,128)S(1)} %copy-done.6, s32[8]{0:T(128)S(1)} %get-tuple-element.22.counts, bf16[2048,512]{1,0:T(8,128)(2,1)S(1)} %copy-done.4, bf16[384,256]{1,0:T(8,128)(2,1)S(1)} %get-tuple-element.23.refs_0_.refs_10_, ...), custom_call_target="tpu_custom_call" | custom-call | flops 6000000000 | bytes 1048576 | tf_op jit(solution)/shard_map/attend_stage/pallas_call | solution.py:528
  24.7 0.0 collective-permute-done.1
  24.7 0.0 collective-permute-done.refs_6_
  24.7 0.1 collective-permute-start.4
  24.8 0.5 collective-permute-start.3
  25.3 1.3 %collective-permute-start.2 = (bf16[2048,128]{1,0:T(8,128)(2,1)S(1)}, bf16[2048,128]{1,0:T(8,128)(2,1)S(1)}, u32[]{:S(2)}, u32[]{:S(2)}) collective-permute-start(bf16[2048,128]{1,0:T(8,128)(2,1)S(1)} %collective-permute-done.refs_6_), channel_id=1, source_target_pairs={{0,4},{4,8},{8,12},{1,5},{5,9},{9,13},{2,6},{6,10},{10,14},{3,7},{... | collective-permute-start | bytes 1572872 | tf_op jit(solution)/shard_map/ppermute | solution.py:26
  26.6 0.2 collective-permute-done.3
  26.9 0.1 maximum_select_fusion.refs_4_.refs_14_
  26.9 0.0 collective-permute-done.4.refs_7_
  26.9 12.8 %attend_stage.4 = (f32[2048,512]{1,0:T(8,128)S(1)}, f32[256,512]{1,0:T(8,128)S(1)}, bf16[384,256]{1,0:T(8,128)(2,1)S(1)}) custom-call(s32[2,8]{1,0:T(2,128)S(1)} %copy-done.6, s32[8]{0:T(128)S(1)} %get-tuple-element.22.counts, bf16[2048,512]{1,0:T(8,128)(2,1)S(1)} %copy-done.4, f32[2048,512]{1,0:T(8,128)S(1)} %get-tuple-element.28.refs_0_, ...), custom_call_target="tpu_custom_call" | custom-call | flops 6000000000 | bytes 1048576 | tf_op jit(solution)/shard_map/attend_stage/pallas_call | solution.py:528
  39.8 0.0 collective-permute-done.2.refs_4_
  39.8 0.2 collective-permute-start.5
  40.0 1.8 %collective-permute-done.5.refs_5_ = bf16[2048,128]{1,0:T(8,128)(2,1)S(1)} collective-permute-done((bf16[2048,128]{1,0:T(8,128)(2,1)S(1)}, bf16[2048,128]{1,0:T(8,128)(2,1)S(1)}, u32[]{:S(2)}, u32[]{:S(2)}) %collective-permute-start.5) | collective-permute-done | bytes 524320 | tf_op jit(solution)/shard_map/ppermute | solution.py:30
  41.7 13.1 %attend_stage.5 = (bf16[2048,512]{1,0:T(8,128)(2,1)}, f32[4,2048]{1,0:T(4,128)}) custom-call(s32[2,8]{1,0:T(2,128)S(1)} %copy-done.6, s32[8]{0:T(128)S(1)} %get-tuple-element.22.counts, bf16[2048,512]{1,0:T(8,128)(2,1)S(1)} %copy-done.4, f32[2048,512]{1,0:T(8,128)S(1)} %get-tuple-element.36.refs_0_, f32[256,512]{1,0:T(8,128)S(1)} %get-tuple-element.37.refs_1_, ...), custom_call_target="tpu_custom_call" | custom-call | flops 6000000000 | bytes 1048576 | tf_op jit(solution)/shard_map/attend_stage/pallas_call | solution.py:528
  (1 shorter events, 0.0 us)
Async XLA Ops:
  1.7 23.0 %collective-permute-start = (bf16[2048,128]{1,0:T(8,128)(2,1)S(1)}, bf16[2048,128]{1,0:T(8,128)(2,1)S(1)}, u32[]{:S(2)}, u32[]{:S(2)}) collective-permute-start(bf16[2048,128]{1,0:T(8,128)(2,1)S(1)} %broadcast_select_fusion), channel_id=1, source_target_pairs={{0,4},{4,8},{8,12},{1,5},{5,9},{9,13},{2,6},{6,10},{10,14},{3,7},{... | collective-permute-start | bytes 1572872 | tf_op jit(solution)/shard_map/ppermute | solution.py:26
  6.7 1.0 %copy-start = (bf16[2048,128]{1,0:T(8,128)(2,1)S(1)}, bf16[2048,128]{1,0:T(8,128)(2,1)}, u32[]{:S(2)}) copy-start(bf16[2048,128]{1,0:T(8,128)(2,1)} %refs_8_.3) | copy-start | bytes 1572868
  7.8 1.0 %copy-start.2 = (bf16[2048,128]{1,0:T(8,128)(2,1)S(1)}, bf16[2048,128]{1,0:T(8,128)(2,1)}, u32[]{:S(2)}) copy-start(bf16[2048,128]{1,0:T(8,128)(2,1)} %refs_9_.3) | copy-start | bytes 1572868
  8.8 0.7 %copy-start.5 = (s32[2,1024]{1,0:T(2,128)S(1)}, s32[2,1024]{1,0:T(2,128)}, u32[]{:S(2)}) copy-start(s32[2,1024]{1,0:T(2,128)} %columns_hbm.1) | copy-start | bytes 24580
  9.5 0.7 %copy-start.6 = (s32[2,8]{1,0:T(2,128)S(1)}, s32[2,8]{1,0:T(2,128)}, u32[]{:S(2)}) copy-start(s32[2,8]{1,0:T(2,128)} %offsets.7) | copy-start | bytes 196
  10.2 5.6 %copy-start.1 = (bf16[2048,128]{1,0:T(8,128)(2,1)S(1)}, bf16[2048,128]{1,0:T(8,128)(2,1)}, u32[]{:S(2)}) copy-start(bf16[2048,128]{1,0:T(8,128)(2,1)} %refs_8_.3) | copy-start | bytes 1572868
  10.2 5.6 %copy-start.3 = (bf16[2048,128]{1,0:T(8,128)(2,1)S(1)}, bf16[2048,128]{1,0:T(8,128)(2,1)}, u32[]{:S(2)}) copy-start(bf16[2048,128]{1,0:T(8,128)(2,1)} %refs_9_.3) | copy-start | bytes 1572868
  10.2 5.6 %copy-start.4 = (bf16[2048,512]{1,0:T(8,128)(2,1)S(1)}, bf16[2048,512]{1,0:T(8,128)(2,1)}, u32[]{:S(2)}) copy-start(bf16[2048,512]{1,0:T(8,128)(2,1)} %q_ref.5) | copy-start | bytes 6291460
  12.5 12.2 %collective-permute-start.1 = (bf16[384,128]{1,0:T(8,128)(2,1)S(1)}, bf16[384,128]{1,0:T(8,128)(2,1)S(1)}, u32[]{:S(2)}, u32[]{:S(2)}) collective-permute-start(bf16[384,128]{1,0:T(8,128)(2,1)S(1)} %slice_select_fusion), channel_id=1, source_target_pairs={{0,12},{1,13},{2,14},{3,15},{16,28},{17,29},{18,30},{19,31}} | collective-permute-start | bytes 294920 | tf_op jit(solution)/shard_map/ppermute | solution.py:26
  24.7 2.2 %collective-permute-start.4 = (bf16[2048,128]{1,0:T(8,128)(2,1)S(1)}, bf16[2048,128]{1,0:T(8,128)(2,1)S(1)}, u32[]{:S(2)}, u32[]{:S(2)}) collective-permute-start(bf16[2048,128]{1,0:T(8,128)(2,1)S(1)} %collective-permute-done.refs_6_), channel_id=1, source_target_pairs={{0,1},{1,0},{2,3},{3,2},{4,5},{5,4},{6,7},{7,6},{8,9},{9,8},{10,11... | collective-permute-start | bytes 1572872 | tf_op jit(solution)/shard_map/ppermute | solution.py:30
  24.8 2.0 %collective-permute-start.3 = (bf16[384,128]{1,0:T(8,128)(2,1)S(1)}, bf16[384,128]{1,0:T(8,128)(2,1)S(1)}, u32[]{:S(2)}, u32[]{:S(2)}) collective-permute-start(bf16[384,128]{1,0:T(8,128)(2,1)S(1)} %collective-permute-done.1), channel_id=1, source_target_pairs={{0,1},{1,0},{2,3},{3,2},{4,5},{5,4},{6,7},{7,6},{8,9},{9,8},{10,11... | collective-permute-start | bytes 294920 | tf_op jit(solution)/shard_map/ppermute | solution.py:30
  25.3 14.4 %collective-permute-start.2 = (bf16[2048,128]{1,0:T(8,128)(2,1)S(1)}, bf16[2048,128]{1,0:T(8,128)(2,1)S(1)}, u32[]{:S(2)}, u32[]{:S(2)}) collective-permute-start(bf16[2048,128]{1,0:T(8,128)(2,1)S(1)} %collective-permute-done.refs_6_), channel_id=1, source_target_pairs={{0,4},{4,8},{8,12},{1,5},{5,9},{9,13},{2,6},{6,10},{10,14},{3,7},{... | collective-permute-start | bytes 1572872 | tf_op jit(solution)/shard_map/ppermute | solution.py:26
  39.8 2.0 %collective-permute-start.5 = (bf16[2048,128]{1,0:T(8,128)(2,1)S(1)}, bf16[2048,128]{1,0:T(8,128)(2,1)S(1)}, u32[]{:S(2)}, u32[]{:S(2)}) collective-permute-start(bf16[2048,128]{1,0:T(8,128)(2,1)S(1)} %collective-permute-done.2.refs_4_), channel_id=1, source_target_pairs={{0,1},{1,0},{2,3},{3,2},{4,5},{5,4},{6,7},{7,6},{8,9},{9,8},{10,11... | collective-permute-start | bytes 1572872 | tf_op jit(solution)/shard_map/ppermute | solution.py:30
